TPU v7x, 256 devices: a whole 4x4x8 slice. The times are simulated.
256 devices in a mesh: gx: 32 (over y, z_lo, core), gy: 8 (over z_hi, x).
Axes of the slice: x: 4, y: 4, z: 8 (z_hi: 2, z_lo: 4; z = z_hi * 4 + z_lo), core: 2. Of those that a mesh axis runs over, the one named last changes fastest.
Arguments:
- populations: float32 [19, 128, 256, 128], P(None, 'gx', 'gy'), may hold values from 0.02 to 0.1
- grain_position: float32 [3, 8192], P(None, 'gx'), may hold values from -6 to 6
- grain_motion: float32 [6, 8192], P(None, 'gx'), may hold values from -0.6 to 0.6
- marker_grain: int32 [524288], P(('gx', 'gy')), may hold values from 0 to 255
- marker_offset: float32 [3, 524288], P(None, ('gx', 'gy')), may hold values from -3 to 3
- marker_weights: float32 [8, 524288], P(None, ('gx', 'gy')), may hold values from 0 to 1, as said below
- marker_cell: int32 [524288], P(('gx', 'gy')), may hold values from 0 to 12158, as said below
- block_dest: int32 [4096], P(('gx', 'gy')), may hold values from 0 to 31, as said below
- bond_pairs: int32 [2, 16384], P(None, 'gx'), may hold values from 0 to 255
- bond_rest: float32 [3, 16384], P(None, 'gx'), may hold values from -6 to 6
Outputs:
- populations_next: float32 [19, 128, 256, 128], P(None, 'gx', 'gy')
- grain_load: float32 [6, 8192], P(None, 'gx')
Inputs may be any that keep to these rules, and one draw needn't show every extreme that they name: A block's markers lie in the fluid brick of gx index block_dest and of the sending device's gy index; no device sends more than 2 of its blocks to one brick. marker_cell = x * 32 * 128 + y * 128 + z with x <= 2, y <= 30, z <= 126, so that the marker's 2 x 2 x 2 stencil lies inside its destination brick. `marker_weights`: each marker's eight weights are nonnegative and sum to one.
All inputs are finite; a program needn't handle non-finite values.
Results may differ from a plain program's by a relative error of at most 0.0003.
Values sent between devices are 32-bit elements; how exact they have to be, the bound alone decides.
No kernel may reach another device: no remote copies, remote signals or barrier semaphores. Data moves between devices by JAX's collectives and lax.ppermute only.
A program may use at most 128 MiB of HBM per device.

v0:
```python
import jax
import jax.numpy as jnp
from jax import lax
from jax.sharding import PartitionSpec as P

MARKS = 128
CAPB = 2


LATTICE = (
    (0, 0, 0),
    (1, 0, 0),
    (-1, 0, 0),
    (0, 1, 0),
    (0, -1, 0),
    (0, 0, 1),
    (0, 0, -1),
    (1, 1, 0),
    (-1, -1, 0),
    (1, -1, 0),
    (-1, 1, 0),
    (1, 0, 1),
    (-1, 0, -1),
    (1, 0, -1),
    (-1, 0, 1),
    (0, 1, 1),
    (0, -1, -1),
    (0, 1, -1),
    (0, -1, 1),
)
OPPOSITE = (0, 2, 1, 4, 3, 6, 5, 8, 7, 10, 9, 12, 11, 14, 13, 16, 15, 18, 17)
RELAX_TIME = 0.8
STIFFNESS = 2.0
MARKER_AREA = 1.0
BOND_SPRING = 1.0
BOND_DAMPING = 0.5
HIGHEST = lax.Precision.HIGHEST


def padded_2(block, sides, width):
    for axis, dim in sides:
        count = lax.axis_size(axis)
        forward = [(i, i + 1) for i in range(count - 1)]
        forward.append((count - 1, 0))
        backward = [(target, source) for source, target in forward]
        low = lax.ppermute(
            lax.slice_in_dim(block, block.shape[dim] - width, None, axis=dim), axis, forward
        )
        high = lax.ppermute(lax.slice_in_dim(block, 0, width, axis=dim), axis, backward)
        block = jnp.concatenate([low, block, high], axis=dim)
    return block


def lattice_weight(vector):
    return (1.0 / 3.0, 1.0 / 18.0, 1.0 / 36.0)[abs(vector[0]) + abs(vector[1]) + abs(vector[2])]


def cross_rows(first_rows, second_rows):
    return jnp.stack(
        [
            first_rows[1] * second_rows[2] - first_rows[2] * second_rows[1],
            first_rows[2] * second_rows[0] - first_rows[0] * second_rows[2],
            first_rows[0] * second_rows[1] - first_rows[1] * second_rows[0],
        ]
    )


def project(vector, field):
    term_list = [
        vector[axis_number] * field[axis_number]
        for axis_number in range(3)
        if vector[axis_number] != 0
    ]
    if not term_list:
        return jnp.zeros_like(field[0])
    return sum(term_list[1:], term_list[0])


def moments(populations):
    density = jnp.sum(populations, axis=0)
    velocity_table = jnp.array(LATTICE, jnp.float32)
    momentum = jnp.einsum("qd,qxyz->dxyz", velocity_table, populations, precision=HIGHEST)
    return (density, momentum)


def collide(populations, density, momentum, forcing):
    velocity = (momentum + 0.5 * forcing) / density
    speed_square = velocity[0] * velocity[0] + velocity[1] * velocity[1] + velocity[2] * velocity[2]
    flow_force = velocity[0] * forcing[0] + velocity[1] * forcing[1] + velocity[2] * forcing[2]
    factor = 1.0 - 0.5 / RELAX_TIME
    result = []
    for number, vector in enumerate(LATTICE):
        weight = lattice_weight(vector)
        along_flow = project(vector, velocity)
        along_force = project(vector, forcing)
        equilibrium = (
            weight
            * density
            * (1.0 + 3.0 * along_flow + 4.5 * along_flow * along_flow - 1.5 * speed_square)
        )
        source = (
            factor * weight * (3.0 * (along_force - flow_force) + 9.0 * along_flow * along_force)
        )
        current = populations[number]
        result.append(current - (current - equilibrium) / RELAX_TIME + source)
    return jnp.stack(result)


def wall_step(shifted, opposite, step_z):
    if step_z == 1:
        return jnp.concatenate([opposite[:, :, :1], shifted[:, :, :-1]], axis=2)
    if step_z == -1:
        return jnp.concatenate([shifted[:, :, 1:], opposite[:, :, -1:]], axis=2)
    return shifted


def corner_tables(cell_flat, weight_flat, size_y, size_z, plane_count, corner_pair):
    step_x, step_y = corner_pair
    plane_row = cell_flat // size_z + step_x * size_y + step_y
    depth = cell_flat % size_z
    plane_onehot = (jnp.arange(plane_count, dtype=jnp.int32)[None, :] == plane_row[:, None]).astype(
        jnp.float32
    )
    depth_grid = jnp.arange(size_z, dtype=jnp.int32)[None, :]
    first = 4 * step_x + 2 * step_y
    depth_weight = jnp.where(depth_grid == depth[:, None], weight_flat[first][:, None], 0.0)
    depth_weight = depth_weight + jnp.where(
        depth_grid == depth[:, None] + 1, weight_flat[first + 1][:, None], 0.0
    )
    return (plane_onehot, depth_weight)


def shards(
    populations,
    grain_position,
    grain_motion,
    marker_grain,
    marker_offset,
    marker_weights,
    marker_cell,
    block_dest,
    bond_pairs,
    bond_rest,
):
    size_x = populations.shape[1]
    size_y = populations.shape[2]
    size_z = populations.shape[3]
    plane_count = size_x * size_y
    density, momentum = moments(populations)
    velocity_rows = jnp.transpose(
        (momentum / density).reshape(3, plane_count, size_z), (1, 0, 2)
    ).reshape(plane_count, 3 * size_z)
    corner_pairs = ((0, 0), (0, 1), (1, 0), (1, 1))
    slab_grains = grain_motion.shape[1]
    marker_count = marker_grain.shape[0]
    block_count = marker_count // MARKS
    brick_count = lax.axis_size("gx")
    owner_table = (
        jnp.arange(slab_grains, dtype=jnp.int32)[:, None] == marker_grain[None, :]
    ).astype(jnp.float32)
    carried = jnp.dot(grain_motion, owner_table, precision=HIGHEST)
    surface = carried[:3] + cross_rows(carried[3:], marker_offset)
    same_brick = block_dest[:, None] == block_dest[None, :]
    earlier = jnp.arange(block_count)[None, :] < jnp.arange(block_count)[:, None]
    rank_in = jnp.sum((same_brick & earlier).astype(jnp.int32), axis=1)
    slot_index = block_dest * CAPB + rank_in
    slot_match = jnp.arange(brick_count * CAPB, dtype=jnp.int32)[:, None] == slot_index[None, :]
    slot_table = slot_match.astype(jnp.float32)
    payload = (
        jnp.concatenate([marker_weights, surface], axis=0)
        .reshape(11, block_count, MARKS)
        .transpose(1, 0, 2)
        .reshape(block_count, 11 * MARKS)
    )
    outgoing = jnp.dot(slot_table, payload, precision=HIGHEST).reshape(brick_count, CAPB, 11, MARKS)
    cell_blocks = marker_cell.reshape(block_count, MARKS)
    cell_outgoing = jnp.sum(jnp.where(slot_match[:, :, None], cell_blocks[None, :, :], 0), axis=1)
    cell_outgoing = cell_outgoing.reshape(brick_count, CAPB, MARKS)
    values = lax.all_to_all(outgoing, "gx", split_axis=0, concat_axis=0, tiled=True)
    cell_ids = lax.all_to_all(cell_outgoing, "gx", split_axis=0, concat_axis=0, tiled=True)
    lead_bricks = values.shape[0]
    lead_items = values.shape[1]
    served = lead_bricks * lead_items * MARKS
    weight_flat = jnp.moveaxis(values[:, :, :8], 2, 0).reshape(8, served)
    target_flat = jnp.moveaxis(values[:, :, 8:], 3, 2).reshape(served, 3)
    cell_flat = cell_ids.reshape(served)
    sampled = jnp.zeros((served, 3), jnp.float32)
    for serve_corner_pair in corner_pairs:
        serve_plane_onehot, serve_depth_weight = corner_tables(
            cell_flat, weight_flat, size_y, size_z, plane_count, serve_corner_pair
        )
        rows = jnp.dot(serve_plane_onehot, velocity_rows, precision=HIGHEST).reshape(
            served, 3, size_z
        )
        sampled = sampled + jnp.sum(rows * serve_depth_weight[:, None, :], axis=2)
    pushed_flat = STIFFNESS * (target_flat - sampled)
    pushed = jnp.moveaxis(pushed_flat.reshape(lead_bricks, lead_items, MARKS, 3), 3, 2)
    returned = lax.all_to_all(pushed, "gx", split_axis=0, concat_axis=0, tiled=True)
    returned, pushed, cell_ids, weights = (returned, pushed, cell_ids, values[:, :, :8])
    received = pushed.shape[0] * pushed.shape[1] * MARKS
    pushed_all = jnp.moveaxis(pushed, 2, 3).reshape(received, 3)
    weight_all = jnp.moveaxis(weights, 2, 0).reshape(8, received)
    cell_all = cell_ids.reshape(received)
    force_rows = jnp.zeros((plane_count, 3 * size_z), jnp.float32)
    for corner_pair in corner_pairs:
        plane_onehot, depth_weight = corner_tables(
            cell_all, weight_all, size_y, size_z, plane_count, corner_pair
        )
        spread_share = (MARKER_AREA * pushed_all[:, :, None] * depth_weight[:, None, :]).reshape(
            received, 3 * size_z
        )
        force_rows = force_rows + lax.dot_general(
            plane_onehot, spread_share, (((0,), (0,)), ((), ())), precision=HIGHEST
        )
    forcing = jnp.transpose(force_rows.reshape(plane_count, 3, size_z), (1, 0, 2)).reshape(
        3, size_x, size_y, size_z
    )
    collided = collide(populations, density, momentum, forcing)
    padded = padded_2(collided, (("gx", 1), ("gy", 2)), 1)
    result = []
    for number, vector in enumerate(LATTICE):
        shifted = padded[
            number,
            1 - vector[0] : 1 - vector[0] + size_x,
            1 - vector[1] : 1 - vector[1] + size_y,
            :,
        ]
        result.append(wall_step(shifted, collided[OPPOSITE[number]], vector[2]))
    populations_next = jnp.stack(result)
    returned_rows = returned.reshape(brick_count * CAPB, 3 * MARKS)
    arrived = lax.dot_general(
        slot_table, returned_rows, (((0,), (0,)), ((), ())), precision=HIGHEST
    ).reshape(block_count, 3, MARKS)
    reaction = -MARKER_AREA * arrived.transpose(1, 0, 2).reshape(3, marker_count)
    marker_load = jnp.concatenate([reaction, cross_rows(marker_offset, reaction)], axis=0)
    partial_value = jnp.dot(marker_load, owner_table.T, precision=HIGHEST)
    first_table = (
        jnp.arange(slab_grains, dtype=jnp.int32)[:, None] == bond_pairs[0][None, :]
    ).astype(jnp.float32)
    second_table = (
        jnp.arange(slab_grains, dtype=jnp.int32)[:, None] == bond_pairs[1][None, :]
    ).astype(jnp.float32)
    bond_state = jnp.concatenate([grain_position, grain_motion[:3]], axis=0)
    first_end = jnp.dot(bond_state, first_table, precision=HIGHEST)
    second_end = jnp.dot(bond_state, second_table, precision=HIGHEST)
    stretch = second_end[:3] - first_end[:3]
    bond_force = BOND_SPRING * (stretch - bond_rest) + BOND_DAMPING * (
        second_end[3:] - first_end[3:]
    )
    bond_torque = 0.5 * cross_rows(stretch, bond_force)
    bonded = jnp.dot(
        jnp.concatenate([bond_force, bond_torque], axis=0), first_table.T, precision=HIGHEST
    )
    bonded = bonded + jnp.dot(
        jnp.concatenate([-bond_force, bond_torque], axis=0), second_table.T, precision=HIGHEST
    )
    hydro_load = lax.psum(partial_value, "gy")
    return (populations_next, hydro_load + bonded)


def solution(mesh):
    in_specs = (
        P(None, "gx", "gy", None),
        P(None, "gx"),
        P(None, "gx"),
        P(("gx", "gy")),
        P(None, ("gx", "gy")),
        P(None, ("gx", "gy")),
        P(("gx", "gy")),
        P(("gx", "gy")),
        P(None, "gx"),
        P(None, "gx"),
    )
    out_specs = (P(None, "gx", "gy", None), P(None, "gx"))
    return jax.shard_map(shards, mesh=mesh, in_specs=in_specs, out_specs=out_specs, check_vma=False)
```

profile of v0, /device:TPU:0, one launch (start us, length us, event | category | flops | bytes accessed | tf_op | source)
XLA Modules:
  0.0 209.6 jit_solution(6158555057406430019)
XLA Ops:
  0.6 1.0 convert_reduce_fusion
  2.4 1.5 select_reduce_fusion
  4.0 7.2 %all-to-all-start = ((s32[32,2,128]{2,1,0:T(2,128)}), s32[32,2,128]{2,1,0:T(2,128)S(1)}, u32[]{:S(2)}, u32[]{:S(2)}) async-start(s32[32,2,128]{2,1,0:T(2,128)} %bitcast.4), calls=%async_computation | async-start | bytes 65536 | tf_op jit(solution)/shard_map/all_to_all | solution.py:180
  12.6 0.9 fusion.44
  13.6 1.0 fusion.45
  14.5 1.5 convolution_bitcast_fusion
  18.5 2.3 %broadcast_divide_fusion = (f32[3,4,32,128]{3,0,2,1:T(4,128)S(1)}, f32[3,4,32,128]{3,0,2,1:T(4,128)}) fusion(f32[4,32,128]{2,1,0:T(8,128)S(1)} %reduce_sum.63, f32[19,3,1,1]{0,1,3,2:T(4,128)S(1)} %copy-done.17, f32[19,4,32,128]{3,2,1,0:T(8,128)S(1)} %copy-done.1), kind=kOutput, calls=%fused_computation.70 | convolution fusion | flops 11255808 | bytes 1704164 | tf_op jit(solution)/shard_map/qd,qxyz->dxyz/dot_general | solution.py:82
  20.9 1.0 copy.150
  21.9 7.9 %all-to-all-start.1 = ((f32[32,2,11,128]{3,1,2,0:T(2,128)}), f32[32,2,11,128]{3,1,2,0:T(2,128)S(1)}, u32[]{:S(2)}, u32[]{:S(2)}) async-start(f32[32,2,11,128]{3,1,2,0:T(2,128)} %copy.150), calls=%async_computation.1 | async-start | bytes 720896 | tf_op jit(solution)/shard_map/all_to_all | solution.py:179
  30.4 12.5 %all-to-all-done.1 = f32[32,2,11,128]{3,1,2,0:T(2,128)S(1)} async-done(((f32[32,2,11,128]{3,1,2,0:T(2,128)}), f32[32,2,11,128]{3,1,2,0:T(2,128)S(1)}, u32[]{:S(2)}, u32[]{:S(2)}) %all-to-all-start.1) | async-done | bytes 360480 | tf_op jit(solution)/shard_map/all_to_all | solution.py:179
  43.1 2.4 %select_add_fusion.2 = (f32[8192,128]{0,1:T(8,128)S(1)}, f32[8192,128]{0,1:T(8,128)S(1)}, f32[8192,128]{0,1:T(8,128)S(1)}, f32[8192,128]{0,1:T(8,128)S(1)}) fusion(f32[8192]{0:T(1024)S(1)} %bitcast.408, f32[8192]{0:T(1024)S(1)} %bitcast.403, s32[8192]{0:T(1024)S(1)} %get-tuple-element.113, s32[8192]{0:T(1024)S(1)} %get-tuple-element.114, ...), kind=kLoop, calls=%fused_computation.16 | loop fusion | flops 14680064 | bytes 17104896 | tf_op jit(solution)/shard_map/add | solution.py:127
  45.5 6.8 %multiply_reduce_fusion.3 = f32[8192,3]{0,1:T(4,128)S(1)} fusion(f32[8192,128]{0,1:T(8,128)S(1)} %get-tuple-element.107, s32[8192]{0:T(1024)S(1)} %get-tuple-element.30, f32[3,128,128]{1,2,0:T(8,128)S(1)} %copy.152), kind=kOutput, calls=%fused_computation.3 | convolution fusion | flops 4839153664 | bytes 4521984 | tf_op jit(solution)/shard_map/dot_general | solution.py:192
  52.3 6.8 %multiply_reduce_fusion.2 = f32[8192,3]{0,1:T(4,128)S(1)} fusion(f32[8192,128]{0,1:T(8,128)S(1)} %get-tuple-element.104, s32[8192]{0:T(1024)S(1)} %get-tuple-element.29, f32[3,128,128]{1,2,0:T(8,128)S(1)} %copy.152), kind=kOutput, calls=%fused_computation.2 | convolution fusion | flops 4839153664 | bytes 4521984 | tf_op jit(solution)/shard_map/dot_general | solution.py:192
  59.1 6.8 %multiply_reduce_fusion = f32[8192,3]{0,1:T(4,128)S(1)} fusion(f32[8192,128]{0,1:T(8,128)S(1)} %get-tuple-element.105, s32[8192]{0:T(1024)S(1)} %get-tuple-element.112, f32[3,128,128]{1,2,0:T(8,128)S(1)} %copy.152), kind=kOutput, calls=%fused_computation | convolution fusion | flops 4839153664 | bytes 4521984 | tf_op jit(solution)/shard_map/dot_general | solution.py:192
  65.9 6.8 %multiply_reduce_fusion.1 = f32[8192,3]{0,1:T(4,128)S(1)} fusion(f32[8192,128]{0,1:T(8,128)S(1)} %get-tuple-element.106, s32[8192]{0:T(1024)S(1)} %get-tuple-element.111, f32[3,128,128]{1,2,0:T(8,128)S(1)} %copy.152), kind=kOutput, calls=%fused_computation.1 | convolution fusion | flops 4839153664 | bytes 4521984 | tf_op jit(solution)/shard_map/dot_general | solution.py:192
  72.9 16.4 %broadcast_multiply_fusion = (f32[8192,3,128]{0,2,1:T(8,128)}, f32[8192,3,128]{0,2,1:T(8,128)}, f32[8192,3,128]{0,2,1:T(8,128)}, f32[8192,3,128]{0,2,1:T(8,128)}) fusion(f32[8192,3]{0,1:T(4,128)S(1)} %get-tuple-element.27, f32[8192,128]{0,1:T(8,128)S(1)} %get-tuple-element.105, f32[8192,128]{0,1:T(8,128)S(1)} %get-tuple-element.104, ...), kind=kLoop, calls=%fused_computation.4 | loop fusion | flops 12582912 | bytes 67207168 | tf_op jit(solution)/shard_map/mul | solution.py:209
  89.2 13.8 %fusion.12 = f32[128,384]{1,0:T(8,128)S(1)} fusion(f32[8192,384]{0,1:T(8,128)} %bitcast.299, s32[8192]{0:T(1024)S(1)} %get-tuple-element.30), kind=kOutput, calls=%fused_computation.27 | convolution fusion | flops 4833935360 | bytes 12812288 | tf_op jit(solution)/shard_map/dot_general | solution.py:212
  103.0 12.7 %fusion.37 = f32[128,384]{1,0:T(8,128)S(1)} fusion(f32[128,384]{1,0:T(8,128)S(1)} %fusion.12, f32[8192,384]{0,1:T(8,128)S(1)} %bitcast.306, s32[8192]{0:T(1024)S(1)} %get-tuple-element.29), kind=kOutput, calls=%fused_computation.45 | convolution fusion | flops 4833984512 | bytes 13008896 | tf_op jit(solution)/shard_map/dot_general | solution.py:212
  115.8 12.7 %fusion.34 = f32[128,384]{1,0:T(8,128)S(1)} fusion(f32[128,384]{1,0:T(8,128)S(1)} %fusion.37, f32[8192,384]{0,1:T(8,128)S(1)} %bitcast.305, s32[8192]{0:T(1024)S(1)} %get-tuple-element.111), kind=kOutput, calls=%fused_computation.44 | convolution fusion | flops 4833984512 | bytes 13008896 | tf_op jit(solution)/shard_map/dot_general | solution.py:212
  128.5 12.9 %fusion.31 = f32[128,384]{1,0:T(8,128)S(1)} fusion(f32[128,384]{1,0:T(8,128)S(1)} %fusion.34, f32[8192,384]{0,1:T(8,128)S(1)} %bitcast.302, s32[8192]{0:T(1024)S(1)} %get-tuple-element.112), kind=kOutput, calls=%fused_computation.43 | convolution fusion | flops 4833984512 | bytes 13008896 | tf_op jit(solution)/shard_map/dot_general | solution.py:212
  142.5 4.5 %all-to-all-start.2 = ((f32[32,2,3,128]{3,1,2,0:T(2,128)}), f32[32,2,3,128]{3,1,2,0:T(2,128)}, u32[]{:S(2)}, u32[]{:S(2)}) async-start(f32[32,2,3,128]{3,1,2,0:T(2,128)} %copy.178), calls=%async_computation.2 | async-start | bytes 196608 | tf_op jit(solution)/shard_map/all_to_all | solution.py:198
  147.9 1.0 copy.233
  151.0 5.5 %collective-permute-start.1 = (f32[19,1,32,128]{3,2,1,0:T(8,128)}, f32[19,1,32,128]{3,2,1,0:T(8,128)S(1)}, u32[]{:S(2)}, u32[]{:S(2)}) collective-permute-start(f32[19,1,32,128]{3,2,1,0:T(8,128)} %get-tuple-element.52), channel_id=1, source_target_pairs={{8,0},{16,8},{24,16},{32,24},{40,32},{48,40},{56,48},{64,56},{72,6... | collective-permute-start | bytes 933896 | tf_op jit(solution)/shard_map/ppermute | solution.py:49
  159.6 0.9 fusion.190
  160.5 0.9 fusion.199
  161.5 0.9 copy.179
  162.7 1.0 fusion.26
  163.7 30.7 %psum.7 = f32[6,256]{1,0:T(8,128)S(1)} all-reduce(f32[6,256]{1,0:T(8,128)S(1)} %fusion.26), channel_id=1, replica_groups=mesh['gx'=32,'gy'=8] {'gy'}, use_global_device_ids=true, to_apply=%region_7.8 | all-reduce | flops 1536 | bytes 12288 | tf_op jit(solution)/shard_map/psum | solution.py:257
  194.5 0.9 fusion.40
  195.6 2.0 collective-permute-start.2
  197.6 8.2 %collective-permute-done.2 = f32[19,6,1,128]{3,2,1,0:T(1,128)S(1)} collective-permute-done((f32[19,6,1,128]{3,2,1,0:T(1,128)S(1)}, f32[19,6,1,128]{3,2,1,0:T(1,128)S(1)}, u32[]{:S(2)}, u32[]{:S(2)}) %collective-permute-start.2) | collective-permute-done | bytes 58400 | tf_op jit(solution)/shard_map/ppermute | solution.py:46
  208.6 1.0 copy-done.3
  (150 shorter events, 15.4 us)
Async XLA Ops:
  0.6 17.3 %copy-start.1 = (f32[19,4,32,128]{3,2,1,0:T(8,128)S(1)}, f32[19,4,32,128]{3,2,1,0:T(8,128)}, u32[]{:S(2)}) copy-start(f32[19,4,32,128]{3,2,1,0:T(8,128)} %param.11) | copy-start | bytes 3735556
  4.0 17.9 %all-to-all-start = ((s32[32,2,128]{2,1,0:T(2,128)}), s32[32,2,128]{2,1,0:T(2,128)S(1)}, u32[]{:S(2)}, u32[]{:S(2)}) async-start(s32[32,2,128]{2,1,0:T(2,128)} %bitcast.4), calls=%async_computation | async-start | bytes 65536 | tf_op jit(solution)/shard_map/all_to_all | solution.py:180
  17.8 0.7 copy-start.17
  18.0 2.8 %copy-start.16 = (f32[3,512]{1,0:T(4,128)S(1)}, f32[3,512]{1,0:T(4,128)}, u32[]{:S(2)}) copy-start(f32[3,512]{1,0:T(4,128)} %param.20) | copy-start | bytes 18436
  21.9 20.9 %all-to-all-start.1 = ((f32[32,2,11,128]{3,1,2,0:T(2,128)}), f32[32,2,11,128]{3,1,2,0:T(2,128)S(1)}, u32[]{:S(2)}, u32[]{:S(2)}) async-start(f32[32,2,11,128]{3,1,2,0:T(2,128)} %copy.150), calls=%async_computation.1 | async-start | bytes 720896 | tf_op jit(solution)/shard_map/all_to_all | solution.py:179
  89.2 13.8 %copy-start = (f32[8192,3,128]{0,2,1:T(8,128)S(1)}, f32[8192,3,128]{0,2,1:T(8,128)}, u32[]{:S(2)}) copy-start(f32[8192,3,128]{0,2,1:T(8,128)} %get-tuple-element.94) | copy-start | bytes 37748740
  89.2 26.5 %slice-start.3 = ((s8[12582912]{0:T(1024)(128)(4,1)}), s8[4194304]{0:T(1024)(128)(4,1)S(1)}, s32[]{:S(2)}) async-start(s8[12582912]{0:T(1024)(128)(4,1)} %bitcast.303), calls=%async_computation.6 | async-start | bytes 8388608
  89.2 26.5 %slice-start.4 = ((s8[12582912]{0:T(1024)(128)(4,1)}), s8[4194304]{0:T(1024)(128)(4,1)S(1)}, s32[]{:S(2)}) async-start(s8[12582912]{0:T(1024)(128)(4,1)} %bitcast.303), calls=%async_computation.7 | async-start | bytes 8388608
  103.0 12.8 %slice-start.5 = ((s8[12582912]{0:T(1024)(128)(4,1)}), s8[4194304]{0:T(1024)(128)(4,1)S(1)}, s32[]{:S(2)}) async-start(s8[12582912]{0:T(1024)(128)(4,1)} %bitcast.303), calls=%async_computation.8 | async-start | bytes 8388608
  103.0 25.5 %slice-start = ((s8[12582912]{0:T(1024)(128)(4,1)}), s8[4194304]{0:T(1024)(128)(4,1)S(1)}, s32[]{:S(2)}) async-start(s8[12582912]{0:T(1024)(128)(4,1)} %bitcast.300), calls=%async_computation.3 | async-start | bytes 8388608
  103.0 25.5 %slice-start.1 = ((s8[12582912]{0:T(1024)(128)(4,1)}), s8[4194304]{0:T(1024)(128)(4,1)S(1)}, s32[]{:S(2)}) async-start(s8[12582912]{0:T(1024)(128)(4,1)} %bitcast.300), calls=%async_computation.4 | async-start | bytes 8388608
  115.8 12.7 %slice-start.2 = ((s8[12582912]{0:T(1024)(128)(4,1)}), s8[4194304]{0:T(1024)(128)(4,1)S(1)}, s32[]{:S(2)}) async-start(s8[12582912]{0:T(1024)(128)(4,1)} %bitcast.300), calls=%async_computation.5 | async-start | bytes 8388608
  141.6 5.9 %copy-start.4 = (f32[3,4,32,128]{3,0,2,1:T(4,128)S(1)}, f32[3,4,32,128]{3,0,2,1:T(4,128)}, u32[]{:S(2)}) copy-start(f32[3,4,32,128]{3,0,2,1:T(4,128)} %get-tuple-element.124) | copy-start | bytes 589828
  142.5 18.9 %all-to-all-start.2 = ((f32[32,2,3,128]{3,1,2,0:T(2,128)}), f32[32,2,3,128]{3,1,2,0:T(2,128)}, u32[]{:S(2)}, u32[]{:S(2)}) async-start(f32[32,2,3,128]{3,1,2,0:T(2,128)} %copy.178), calls=%async_computation.2 | async-start | bytes 196608 | tf_op jit(solution)/shard_map/all_to_all | solution.py:198
  151.0 44.4 %collective-permute-start.1 = (f32[19,1,32,128]{3,2,1,0:T(8,128)}, f32[19,1,32,128]{3,2,1,0:T(8,128)S(1)}, u32[]{:S(2)}, u32[]{:S(2)}) collective-permute-start(f32[19,1,32,128]{3,2,1,0:T(8,128)} %get-tuple-element.52), channel_id=1, source_target_pairs={{8,0},{16,8},{24,16},{32,24},{40,32},{48,40},{56,48},{64,56},{72,6... | collective-permute-start | bytes 933896 | tf_op jit(solution)/shard_map/ppermute | solution.py:49
  156.5 39.0 %collective-permute-start = (f32[19,1,32,128]{3,2,1,0:T(8,128)}, f32[19,1,32,128]{3,2,1,0:T(8,128)S(1)}, u32[]{:S(2)}, u32[]{:S(2)}) collective-permute-start(f32[19,1,32,128]{3,2,1,0:T(8,128)} %get-tuple-element.53), channel_id=1, source_target_pairs={{0,8},{8,16},{16,24},{24,32},{32,40},{40,48},{48,56},{56,64},{64,7... | collective-permute-start | bytes 933896 | tf_op jit(solution)/shard_map/ppermute | solution.py:46
  159.6 3.0 %copy-start.15 = (f32[3,2048]{1,0:T(4,128)S(1)}, f32[3,2048]{1,0:T(4,128)}, u32[]{:S(2)}) copy-start(f32[3,2048]{1,0:T(4,128)} %param.15) | copy-start | bytes 73732
  159.6 3.1 %copy-start.18 = (s32[2048]{0:T(1024)S(1)}, s32[2048]{0:T(1024)}, u32[]{:S(2)}) copy-start(s32[2048]{0:T(1024)} %param.14) | copy-start | bytes 24580
  162.7 34.9 %copy-start.2 = (f32[19,4,32,128]{3,2,1,0:T(8,128)S(1)}, f32[19,4,32,128]{3,2,1,0:T(8,128)}, u32[]{:S(2)}) copy-start(f32[19,4,32,128]{3,2,1,0:T(8,128)} %copy.233) | copy-start | bytes 3735556
  195.5 10.4 %collective-permute-start.3 = (f32[19,6,1,128]{3,2,1,0:T(1,128)S(1)}, f32[19,6,1,128]{3,2,1,0:T(1,128)S(1)}, u32[]{:S(2)}, u32[]{:S(2)}) collective-permute-start(f32[19,6,1,128]{3,2,1,0:T(1,128)S(1)} %get-tuple-element.37), channel_id=1, source_target_pairs={{1,0},{2,1},{3,2},{4,3},{5,4},{6,5},{7,6},{0,7},{9,8},{10,9},{11,1... | collective-permute-start | bytes 175112 | tf_op jit(solution)/shard_map/ppermute | solution.py:49
  195.6 10.3 %collective-permute-start.2 = (f32[19,6,1,128]{3,2,1,0:T(1,128)S(1)}, f32[19,6,1,128]{3,2,1,0:T(1,128)S(1)}, u32[]{:S(2)}, u32[]{:S(2)}) collective-permute-start(f32[19,6,1,128]{3,2,1,0:T(1,128)S(1)} %get-tuple-element.38), channel_id=1, source_target_pairs={{0,1},{1,2},{2,3},{3,4},{4,5},{5,6},{6,7},{7,0},{8,9},{9,10},{10,1... | collective-permute-start | bytes 175112 | tf_op jit(solution)/shard_map/ppermute | solution.py:46
  205.9 0.8 copy-start.13
  205.9 0.9 copy-start.14
  207.0 0.8 copy-start.9
  207.0 0.9 copy-start.12
  207.0 1.0 copy-start.10
  207.0 1.1 copy-start.8
  207.0 1.2 copy-start.6
  207.0 1.3 copy-start.11
  207.0 1.3 copy-start.7
  207.1 1.4 copy-start.5
  208.6 1.0 copy-start.3
where the time goes:
time: 211 us; the launch traced here: 210 us
  matrix products  88 us (42%)
  blocking collectives  30.7 us (15%)
  other arithmetic  30 us (14%)
  starting transfers between devices  27.2 us (13%)
  waiting for transfers between devices  20.7 us (10%)
  local copies, waits for them, and re-layouts  11.5 us (5%)
    dot_general x4, matrix products, shards(): lax.dot_general(plane_onehot, spread_share, (((0,), (0,)), ((), ())), pre...  52.1 us
    psum x1, blocking collectives, shards(): hydro_load = lax.psum(partial_value, 'gy')  30.7 us
    dot_general x4, matrix products, shards(): jnp.dot(serve_plane_onehot, velocity_rows, precision=HIGHEST)  27.2 us
    mul x1, other arithmetic, shards(): MARKER_AREA * pushed_all[:, :, None] * depth_weight[:, None, :]  16.4 us
    all_to_all x1, waiting for transfers between devices, shards(): lax.all_to_all(outgoing, 'gx', split_axis=0, concat_axis=0, tiled=True)  12.5 us
    ppermute x2, waiting for transfers between devices, padded_2(): lax.ppermute(lax.slice_in_dim(block, block.shape[dim] - width, None, axis...  8.25 us
    all_to_all x1, starting transfers between devices, shards(): lax.all_to_all(outgoing, 'gx', split_axis=0, concat_axis=0, tiled=True)  7.87 us
    all_to_all x1, starting transfers between devices, shards(): lax.all_to_all(cell_outgoing, 'gx', split_axis=0, concat_axis=0, tiled=True)  7.19 us
  transfers between devices with their start and end apart: 7, of which 2 were waited for; matrix products, arithmetic and copies ran while one was open for 11% of the time, Pallas kernels for 0%

commit v1 on v0

v1 whole, which is shorter than its diff:
```python
import jax
import jax.numpy as jnp
from jax import lax
from jax.experimental import pallas as pl
from jax.experimental.pallas import tpu as pltpu
from jax.sharding import PartitionSpec as P

MARKS = 128
CAPB = 2
SLOT_ROWS = 24
BACK_ROWS = 8
EDGE_ROWS = 24
UNROLL = 8
REDUCE_STEPS = ((1, 2, 3), (4,))


LATTICE = (
    (0, 0, 0),
    (1, 0, 0),
    (-1, 0, 0),
    (0, 1, 0),
    (0, -1, 0),
    (0, 0, 1),
    (0, 0, -1),
    (1, 1, 0),
    (-1, -1, 0),
    (1, -1, 0),
    (-1, 1, 0),
    (1, 0, 1),
    (-1, 0, -1),
    (1, 0, -1),
    (-1, 0, 1),
    (0, 1, 1),
    (0, -1, -1),
    (0, 1, -1),
    (0, -1, 1),
)
OPPOSITE = (0, 2, 1, 4, 3, 6, 5, 8, 7, 10, 9, 12, 11, 14, 13, 16, 15, 18, 17)
RELAX_TIME = 0.8
STIFFNESS = 2.0
MARKER_AREA = 1.0
BOND_SPRING = 1.0
BOND_DAMPING = 0.5
UP_X = tuple(i for i, v in enumerate(LATTICE) if v[0] == 1)
DOWN_X = tuple(i for i, v in enumerate(LATTICE) if v[0] == -1)
UP_Y = tuple(i for i, v in enumerate(LATTICE) if v[1] == 1)
DOWN_Y = tuple(i for i, v in enumerate(LATTICE) if v[1] == -1)
NT = (((1,), (1,)), ((), ()))
NN = (((1,), (0,)), ((), ()))
VMEM = pl.BlockSpec(memory_space=pltpu.VMEM)
SMEM = pl.BlockSpec(memory_space=pltpu.SMEM)
HBM = pl.BlockSpec(memory_space=pltpu.HBM)
ANYWHERE = pl.BlockSpec(memory_space=pl.ANY)
F32 = jnp.float32
BF16 = jnp.bfloat16


def lattice_weight(vector):
    return (1.0 / 3.0, 1.0 / 18.0, 1.0 / 36.0)[abs(vector[0]) + abs(vector[1]) + abs(vector[2])]


def cross_rows(first_rows, second_rows):
    return [
        first_rows[1] * second_rows[2] - first_rows[2] * second_rows[1],
        first_rows[2] * second_rows[0] - first_rows[0] * second_rows[2],
        first_rows[0] * second_rows[1] - first_rows[1] * second_rows[0],
    ]


def rows_of(array):
    return [array[i : i + 1] for i in range(array.shape[0])]


def halves(value):
    high = value.astype(BF16)
    low = (value - high.astype(F32)).astype(BF16)
    return high, low


def thirds(value):
    high = value.astype(BF16)
    rest = value - high.astype(F32)
    middle = rest.astype(BF16)
    return high, middle, (rest - middle.astype(F32)).astype(BF16)


def one_hot(count, index_row):
    lanes = index_row.shape[1]
    grid = lax.broadcasted_iota(jnp.int32, (count, lanes), 0)
    return jnp.where(grid == index_row, 1.0, 0.0).astype(BF16)


def pick(state, table, dims):
    rows = state.shape[0]
    stacked = jnp.concatenate([t.astype(F32) for t in thirds(state)], axis=0).astype(BF16)
    got = lax.dot_general(stacked, table, dims, preferred_element_type=F32)
    return got[:rows] + got[rows : 2 * rows] + got[2 * rows :]


def pad_rows(value, rows):
    return jnp.concatenate([value, jnp.zeros((rows - value.shape[0], value.shape[1]), F32)], axis=0)


def fetch(sources, targets, sems):
    copies = [
        pltpu.make_async_copy(source, target, sems.at[index])
        for index, (source, target) in enumerate(zip(sources, targets))
    ]
    for copy in copies:
        copy.start()
    return copies


def pack_kernel(*refs):
    sources, (out, used, sems), held = refs[:6], refs[6:9], refs[9:]
    copies = fetch(sources, held, sems)
    dest, grain, cell, motion, offset, weights = held
    blocks = grain.shape[0]
    slab = motion.shape[1]
    out[...] = jnp.zeros_like(out)
    for brick in range(out.shape[0]):
        used[brick] = 0
    for copy in copies:
        copy.wait()
    state = pad_rows(motion[...], 8)
    half = lax.broadcasted_iota(jnp.int32, (8, MARKS), 0) // 4
    for block in range(blocks):
        span = slice(block * MARKS, (block + 1) * MARKS)
        carried = pick(state, one_hot(slab, grain[block : block + 1, :]), NN)
        moved = rows_of(carried)
        lever = rows_of(offset[:, span])
        turned = cross_rows(moved[3:6], lever)
        tail = [moved[i] + turned[i] for i in range(3)]
        tail.append(cell[block : block + 1, :].astype(F32))
        tail = jnp.concatenate(tail + tail, axis=0)
        brick = dest[block]
        slot = used[brick]
        used[brick] = slot + 1
        out[brick, pl.ds(pl.multiple_of(8 * slot, 8), 8), :] = weights[:, span]
        out[brick, 16:24, :] = jnp.where(half == slot, tail, out[brick, 16:24, :])


def bond_part(pairs, rest, position, motion, bonded):
    slab = position.shape[1]
    state = pad_rows(jnp.concatenate([position[...], motion[0:3, :]], axis=0), 8)
    first = one_hot(slab, pairs[0:1, :])
    second = one_hot(slab, pairs[1:2, :])
    near = pick(state, first, NN)
    far = pick(state, second, NN)
    stretch = far[:3] - near[:3]
    force = BOND_SPRING * (stretch - rest[...]) + BOND_DAMPING * (far[3:6] - near[3:6])
    torque = [0.5 * row for row in cross_rows(rows_of(stretch), rows_of(force))]
    torque = jnp.concatenate(torque, axis=0)
    blank = jnp.zeros((2, force.shape[1]), F32)
    total = pick(jnp.concatenate([force, torque, blank], axis=0), first, NT)
    total = total + pick(jnp.concatenate([-force, torque, blank], axis=0), second, NT)
    bonded[...] = total


def momentum_of(current):
    total = []
    for axis in range(3):
        value = None
        for number, vector in enumerate(LATTICE):
            if vector[axis] == 0:
                continue
            if value is None:
                value = current[number] if vector[axis] == 1 else -current[number]
            elif vector[axis] == 1:
                value = value + current[number]
            else:
                value = value - current[number]
        total.append(value)
    return total


def sum_of(values):
    values = list(values)
    while len(values) > 1:
        values = [
            values[i] + values[i + 1] if i + 1 < len(values) else values[i]
            for i in range(0, len(values), 2)
        ]
    return values[0]


def moment_kernel(populations, pairs, rest, position, motion, table, bonded):
    quantity, size_x, size_y, size_z = populations.shape
    planes = size_x * size_y
    for x in range(size_x):
        current = [populations[q, x] for q in range(quantity)]
        inverse = 1.0 / sum_of(current)
        for axis, value in enumerate(momentum_of(current)):
            speed = value * inverse
            for step in range(2):
                if step == 1:
                    speed = pltpu.roll(speed, size_z - 1, 1)
                high, low = halves(speed)
                first = (step * 3 + axis) * planes + x * size_y
                table[first : first + size_y, 0:size_z] = high
                table[first : first + size_y, size_z : 2 * size_z] = low
    bond_part(pairs, rest, position, motion, bonded)


def marker_tables(slots, size_x, size_y, size_z):
    cells = jnp.concatenate([slots[19:20], slots[23:24]], axis=1).astype(jnp.int32)
    weight = jnp.concatenate([slots[0:8], slots[8:16]], axis=1)
    place_x = lax.shift_right_logical(cells, (size_y * size_z).bit_length() - 1)
    place_y = lax.shift_right_logical(cells, size_z.bit_length() - 1) & (size_y - 1)
    place_z = cells & (size_z - 1)
    depth = one_hot(size_z, place_z)
    row = lax.broadcasted_iota(jnp.int32, (size_y, cells.shape[1]), 0)
    at_low = row == place_y
    at_high = row == place_y + 1
    shares = [[None] * size_x, [None] * size_x]
    for x in range(size_x):
        share = jnp.where(place_x == x - 1, weight[4:8], 0.0)
        share = jnp.where(place_x == x, weight[0:4], share)
        for step in range(2):
            value = jnp.where(at_high, share[2 + step : 3 + step], 0.0)
            shares[step][x] = jnp.where(at_low, share[step : step + 1], value)
    return depth, shares


def sample_kernel(slots, table, pushed, *, size):
    size_x, size_y, size_z = size
    planes = size_x * size_y

    def body(source, carry):
        rows = slots[source]
        depth, shares = marker_tables(rows, size_x, size_y, size_z)
        found = lax.dot_general(
            table[...],
            jnp.concatenate([depth, depth], axis=0),
            NN,
            preferred_element_type=F32,
        )
        target = jnp.concatenate([rows[16:19], rows[20:23]], axis=1)
        force = []
        for axis in range(3):
            value = None
            for step in range(2):
                for x in range(size_x):
                    first = (step * 3 + axis) * planes + x * size_y
                    term = shares[step][x] * found[first : first + size_y]
                    value = term if value is None else value + term
            sampled = jnp.sum(value, axis=0, keepdims=True)
            force.append(STIFFNESS * (target[axis : axis + 1] - sampled))
        blank = jnp.zeros_like(force[0])
        force = jnp.concatenate(force + [blank], axis=0)
        pushed[source] = jnp.concatenate([force[:, :MARKS], force[:, MARKS:]], axis=0)
        return carry

    lax.fori_loop(0, slots.shape[0], body, 0, unroll=UNROLL)


def spread_kernel(
    place, slots, pushed, populations, collided, near_x, far_x, near_y, far_y, total
):
    quantity, size_x, size_y, size_z = populations.shape
    planes = size_x * size_y
    total[...] = jnp.zeros_like(total)

    def body(source, carry):
        depth, shares = marker_tables(slots[source], size_x, size_y, size_z)
        both = pushed[source]
        force = jnp.concatenate([both[0:4], both[4:8]], axis=1)
        high = []
        low = []
        for step in range(2):
            for axis in range(3):
                for x in range(size_x):
                    one, two = halves(MARKER_AREA * force[axis : axis + 1] * shares[step][x])
                    high.append(one)
                    low.append(two)
        left = jnp.concatenate(
            [jnp.concatenate(high, axis=0), jnp.concatenate(low, axis=0)], axis=1
        )
        right = jnp.concatenate([depth, depth], axis=1)
        total[...] += lax.dot_general(left, right, NT, preferred_element_type=F32)
        return carry

    lax.fori_loop(0, slots.shape[0], body, 0, unroll=UNROLL)

    factor = 1.0 - 0.5 / RELAX_TIME
    for x in range(size_x):
        current = [populations[q, x] for q in range(quantity)]
        density = sum_of(current)
        inverse = 1.0 / density
        momentum = momentum_of(current)
        forcing = []
        for axis in range(3):
            first = axis * planes + x * size_y
            near = total[first : first + size_y]
            far = total[3 * planes + first : 3 * planes + first + size_y]
            forcing.append(near + pltpu.roll(far, 1, 1))
        velocity = [(momentum[a] + 0.5 * forcing[a]) * inverse for a in range(3)]
        speed_square = sum_of([v * v for v in velocity])
        flow_force = sum_of([velocity[a] * forcing[a] for a in range(3)])
        rest_flow = 1.0 - 1.5 * speed_square
        rest_force = -3.0 * flow_force
        for number, vector in enumerate(LATTICE):
            weight = lattice_weight(vector)
            flow = rest_flow
            push = rest_force
            if any(vector):
                along_flow = project(vector, velocity)
                along_force = project(vector, forcing)
                flow = flow + along_flow * (3.0 + 4.5 * along_flow)
                push = push + along_force * (3.0 + 9.0 * along_flow)
            value = (
                (1.0 - 1.0 / RELAX_TIME) * current[number]
                + (weight / RELAX_TIME) * density * flow
                + (factor * weight) * push
            )
            collided[number, x] = value
            if x == size_x - 1 and number in UP_X:
                put_face(place[0] == 0, near_x, far_x, UP_X.index(number), value)
            if x == 0 and number in DOWN_X:
                put_face(place[0] == 1, near_x, far_x, DOWN_X.index(number), value)
            if number in UP_Y:
                line = UP_Y.index(number) * size_x + x
                put_row(place[1] == 0, near_y, far_y, line, value[size_y - 1 : size_y])
            if number in DOWN_Y:
                line = DOWN_Y.index(number) * size_x + x
                put_row(place[1] == 1, near_y, far_y, line, value[0:1])
    filled = len(UP_Y) * size_x
    for face in (near_y, far_y):
        face[filled:] = jnp.zeros_like(face[filled:])


def put_face(to_near, near, far, index, value):
    @pl.when(to_near)
    def _():
        near[index] = value

    @pl.when(jnp.logical_not(to_near))
    def _():
        far[index] = value


def put_row(to_near, near, far, line, value):
    @pl.when(to_near)
    def _():
        near[line : line + 1] = value

    @pl.when(jnp.logical_not(to_near))
    def _():
        far[line : line + 1] = value


def edge_kernel(
    place, near_x, far_x, near_y, far_y, *refs, size_x
):
    parts, (near_out, far_out, total_out) = refs[:-3], refs[-3:]
    size_y = near_x.shape[1]
    filled = len(UP_Y) * size_x
    even_x = place[0] == 0
    from_x = lambda number, y: jnp.where(
        even_x, far_x[UP_X.index(number), y : y + 1], near_x[UP_X.index(number), y : y + 1]
    )
    to_x = lambda number, y: jnp.where(
        even_x, near_x[DOWN_X.index(number), y : y + 1], far_x[DOWN_X.index(number), y : y + 1]
    )
    top = size_y - 1
    up = jnp.concatenate([from_x(LATTICE.index((1, 1, 0)), top), to_x(LATTICE.index((-1, 1, 0)), top)], axis=0)
    down = jnp.concatenate([from_x(LATTICE.index((1, -1, 0)), 0), to_x(LATTICE.index((-1, -1, 0)), 0)], axis=0)
    even_y = place[1] == 0
    near_out[...] = near_y[...]
    far_out[...] = far_y[...]
    near_out[filled : filled + 2] = jnp.where(even_y, up, down)
    far_out[filled : filled + 2] = jnp.where(even_y, down, up)
    total_out[...] = sum_of([part[...] for part in parts])


def project(vector, field):
    value = None
    for axis in range(3):
        if vector[axis] == 0:
            continue
        if value is None:
            value = field[axis] if vector[axis] == 1 else -field[axis]
        elif vector[axis] == 1:
            value = value + field[axis]
        else:
            value = value - field[axis]
    return value


def stream_kernel(
    place, collided, near_x, far_x, near_y, far_y, *refs
):
    parts, (out, load, stage, sems) = refs[:-4], refs[-4:]
    quantity, size_x, size_y, size_z = collided.shape
    row = lax.broadcasted_iota(jnp.int32, (size_y, size_z), 0)
    lane = lax.broadcasted_iota(jnp.int32, (size_y, size_z), 1)
    even_x = place[0] == 0
    even_y = place[1] == 0
    filled = len(UP_Y) * size_x
    from_y = jnp.where(even_y, far_y[...], near_y[...])
    to_y = jnp.where(even_y, near_y[...], far_y[...])
    copies = []
    for x in (1, 2, 0, 3):
        for number, vector in enumerate(LATTICE):
            source = x - vector[0]
            inside = 0 <= source < size_x
            if inside:
                value = collided[number, source]
            elif vector[0] == 1:
                index = UP_X.index(number)
                value = jnp.where(even_x, far_x[index], near_x[index])
            else:
                index = DOWN_X.index(number)
                value = jnp.where(even_x, near_x[index], far_x[index])
            if vector[1]:
                face = from_y if vector[1] == 1 else to_y
                column = UP_Y if vector[1] == 1 else DOWN_Y
                if inside:
                    line = column.index(number) * size_x + source
                else:
                    line = filled if vector[0] == 1 else filled + 1
                ghost = face[line : line + 1]
                if vector[1] == 1:
                    value = jnp.where(row == 0, ghost, pltpu.roll(value, 1, 0))
                else:
                    value = jnp.where(row == size_y - 1, ghost, pltpu.roll(value, size_y - 1, 0))
            if vector[2]:
                back = collided[OPPOSITE[number], x]
                if vector[2] == 1:
                    value = jnp.where(lane == 0, back, pltpu.roll(value, 1, 1))
                else:
                    value = jnp.where(lane == size_z - 1, back, pltpu.roll(value, size_z - 1, 1))
            stage[number, x] = value
        copy = pltpu.make_async_copy(stage.at[:, x], out.at[:, x], sems.at[x])
        copy.start()
        copies.append(copy)
    total = sum_of([part[...] for part in parts])
    load[...] = total[: load.shape[0]]
    for copy in copies:
        copy.wait()


def grain_kernel(dest, grain, offset, returned, after, partial, used):
    blocks = grain.shape[0]
    slab = partial.shape[1]
    for brick in range(returned.shape[0]):
        used[brick] = 0
    total = None
    for block in range(blocks):
        span = slice(block * MARKS, (block + 1) * MARKS)
        brick = dest[block]
        slot = used[brick]
        used[brick] = slot + 1
        both = returned[brick]
        force = jnp.where(slot == 0, both[0:3], both[4:7])
        reaction = -MARKER_AREA * force
        torque = cross_rows(rows_of(offset[:, span]), rows_of(reaction))
        load = jnp.concatenate([reaction] + torque + [jnp.zeros((2, MARKS), F32)], axis=0)
        term = pick(load, one_hot(slab, grain[block : block + 1, :]), NT)
        total = term if total is None else total + term
    partial[...] = total


def cross(step):
    return [(i, i ^ step) for i in range(lax.axis_size("gy"))]


def swap(axis, step):
    count = lax.axis_size(axis)
    return [(i, (i + 1 if i % 2 == step else i - 1) % count) for i in range(count)]


def shards(
    populations,
    grain_position,
    grain_motion,
    marker_grain,
    marker_offset,
    marker_weights,
    marker_cell,
    block_dest,
    bond_pairs,
    bond_rest,
):
    quantity, size_x, size_y, size_z = populations.shape
    planes = size_x * size_y
    slab = grain_motion.shape[1]
    blocks = marker_grain.shape[0] // MARKS
    bricks = lax.axis_size("gx")
    shape = jax.ShapeDtypeStruct
    params = pltpu.CompilerParams(vmem_limit_bytes=48 * 1024 * 1024)
    grain_blocks = marker_grain.reshape(blocks, MARKS)
    cell_blocks = marker_cell.reshape(blocks, MARKS)

    place = jnp.stack([lax.axis_index("gx") & 1, lax.axis_index("gy") & 1]).astype(jnp.int32)
    outgoing = pl.pallas_call(
        pack_kernel,
        out_shape=shape((bricks, SLOT_ROWS, MARKS), F32),
        in_specs=[HBM] * 6,
        out_specs=VMEM,
        scratch_shapes=[
            pltpu.SMEM((bricks,), jnp.int32),
            pltpu.SemaphoreType.DMA((6,)),
            pltpu.SMEM(block_dest.shape, jnp.int32),
            pltpu.VMEM(grain_blocks.shape, jnp.int32),
            pltpu.VMEM(cell_blocks.shape, jnp.int32),
            pltpu.VMEM(grain_motion.shape, F32),
            pltpu.VMEM(marker_offset.shape, F32),
            pltpu.VMEM(marker_weights.shape, F32),
        ],
        compiler_params=params,
        name="pack",
    )(
        *[
            pltpu.with_memory_space_constraint(array, pltpu.HBM)
            for array in (
                block_dest,
                grain_blocks,
                cell_blocks,
                grain_motion,
                marker_offset,
                marker_weights,
            )
        ]
    )
    slots = lax.all_to_all(outgoing, "gx", split_axis=0, concat_axis=0, tiled=True)

    table, bonded = pl.pallas_call(
        moment_kernel,
        out_shape=[shape((6 * planes, 2 * size_z), BF16), shape((8, slab), F32)],
        in_specs=[VMEM] * 5,
        out_specs=[VMEM] * 2,
        compiler_params=params,
        cost_estimate=pl.CostEstimate(flops=20000000, bytes_accessed=4000000, transcendentals=0),
        name="moments",
    )(populations, bond_pairs, bond_rest, grain_position, grain_motion)

    pushed = pl.pallas_call(
        lambda *refs: sample_kernel(*refs, size=(size_x, size_y, size_z)),
        out_shape=shape((bricks, BACK_ROWS, MARKS), F32),
        in_specs=[VMEM] * 2,
        out_specs=VMEM,
        compiler_params=params,
        name="sample",
    )(slots, table)
    returned = lax.all_to_all(pushed, "gx", split_axis=0, concat_axis=0, tiled=True)

    collided, *faces = pl.pallas_call(
        spread_kernel,
        out_shape=[
            shape(populations.shape, F32),
            shape((len(UP_X), size_y, size_z), F32),
            shape((len(UP_X), size_y, size_z), F32),
            shape((EDGE_ROWS, size_z), F32),
            shape((EDGE_ROWS, size_z), F32),
        ],
        in_specs=[SMEM] + [VMEM] * 3,
        out_specs=[VMEM] * 5,
        scratch_shapes=[pltpu.VMEM((6 * planes, size_z), F32)],
        compiler_params=params,
        cost_estimate=pl.CostEstimate(
            flops=6000000000, bytes_accessed=8000000, transcendentals=0
        ),
        name="spread",
    )(place, slots, pushed, populations)

    near_x = lax.ppermute(faces[0], "gx", swap("gx", 0))
    far_x = lax.ppermute(faces[1], "gx", swap("gx", 1))

    partial = pl.pallas_call(
        grain_kernel,
        out_shape=shape((8, slab), F32),
        in_specs=[SMEM] + [VMEM] * 3 + [ANYWHERE],
        out_specs=VMEM,
        scratch_shapes=[pltpu.SMEM((bricks,), jnp.int32)],
        compiler_params=params,
        name="grain",
    )(block_dest, grain_blocks, marker_offset, returned, faces[2])
    first, second = REDUCE_STEPS
    parts = [partial] + [lax.ppermute(partial, "gy", cross(step)) for step in first]

    near_y, far_y, total = pl.pallas_call(
        lambda *refs: edge_kernel(*refs, size_x=size_x),
        out_shape=[shape((EDGE_ROWS, size_z), F32)] * 2 + [shape((8, slab), F32)],
        in_specs=[SMEM] + [VMEM] * (4 + len(parts)),
        out_specs=[VMEM] * 3,
        compiler_params=params,
        name="edge",
    )(place, near_x, far_x, faces[2], faces[3], *parts)
    near_y = lax.ppermute(near_y, "gy", swap("gy", 0))
    far_y = lax.ppermute(far_y, "gy", swap("gy", 1))
    parts = [bonded, total] + [lax.ppermute(total, "gy", cross(step)) for step in second]

    populations_next, grain_load = pl.pallas_call(
        stream_kernel,
        out_shape=[shape(populations.shape, F32), shape((6, slab), F32)],
        in_specs=[SMEM] + [VMEM] * (5 + len(parts)),
        out_specs=[ANYWHERE, VMEM],
        scratch_shapes=[
            pltpu.VMEM(populations.shape, F32),
            pltpu.SemaphoreType.DMA((size_x,)),
        ],
        compiler_params=params,
        name="stream",
    )(place, collided, near_x, far_x, near_y, far_y, *parts)
    return populations_next, grain_load


def solution(mesh):
    in_specs = (
        P(None, "gx", "gy", None),
        P(None, "gx"),
        P(None, "gx"),
        P(("gx", "gy")),
        P(None, ("gx", "gy")),
        P(None, ("gx", "gy")),
        P(("gx", "gy")),
        P(("gx", "gy")),
        P(None, "gx"),
        P(None, "gx"),
    )
    out_specs = (P(None, "gx", "gy", None), P(None, "gx"))
    return jax.shard_map(shards, mesh=mesh, in_specs=in_specs, out_specs=out_specs, check_vma=False)
```

time: 211 us -> 76 us (0.36)
  matrix products: 88 us -> 0 us
  blocking collectives: 30.7 us -> 0 us
  other arithmetic: 30 us -> 0.08 us
  Pallas kernels: 0 us -> 22.4 us
  local copies, waits for them, and re-layouts: 11.5 us -> 0.04 us
  waiting for transfers between devices: 20.7 us -> 23.1 us
    dot_general x17 -> x0, matrix products: 88 us -> none  [the longest x4 52.1 us: shards(): lax.dot_general(plane_onehot, spread_share, (((0,), (0,)), ((), ())), pre...]
    psum x1 -> x0, blocking collectives: 30.7 us -> none  [shards(): hydro_load = lax.psum(partial_value, 'gy')]
    pallas_call x0 -> x7, Pallas kernels: none -> 22.4 us  [the longest x1 10.1 us: shards(): pl.pallas_call(spread_kernel, out_shape=[shape(populations.shape, F32), s...]
    mul x4 -> x0, other arithmetic: 16.5 us -> none  [the longest x1 16.4 us: shards(): MARKER_AREA * pushed_all[:, :, None] * depth_weight[:, None, :]]
    ppermute x4 -> x8, starting transfers between devices: 7.57 us -> 18.2 us  [the longest x1 6.24 us: shards(): far_y = lax.ppermute(far_y, 'gy', swap('gy', 1))]
    all_to_all x1 -> x0, starting transfers between devices: 7.19 us -> none  [shards(): lax.all_to_all(cell_outgoing, 'gx', split_axis=0, concat_axis=0, tiled=True)]
    add x12 -> x0, other arithmetic: 6.78 us -> none  [the longest x6 3.39 us: collide(): result.append(current - (current - equilibrium) / RELAX_TIME + source)]
    slice x16 -> x0, local copies, waits for them, and re-layouts: 4.64 us -> none  [the longest x6 1.75 us: wall_step(): return jnp.concatenate([shifted[:, :, 1:], opposite[:, :, -1:]], axis=2)]
  transfers between devices with their start and end apart: 7 -> 10, of which waited for: 2 -> 4; matrix products, arithmetic and copies ran while one was open for 11% -> 0% of each run, Pallas kernels for 0% -> 15%
where the time goes in v1:
time: 76 us; the launch traced here: 75.7 us
  starting transfers between devices  29.2 us (38%)
  waiting for transfers between devices  23.1 us (30%)
  Pallas kernels  22.4 us (29%)
  between operations  0.81 us (1%)
    all_to_all x1, waiting for transfers between devices, shards(): lax.all_to_all(outgoing, 'gx', split_axis=0, concat_axis=0, tiled=True)  13.2 us
    pallas_call x1, Pallas kernels, shards(): pl.pallas_call(spread_kernel, out_shape=[shape(populations.shape, F32), s...  10.1 us
    all_to_all x1, starting transfers between devices, shards(): lax.all_to_all(outgoing, 'gx', split_axis=0, concat_axis=0, tiled=True)  7.2 us
    ppermute x1, starting transfers between devices, shards(): far_y = lax.ppermute(far_y, 'gy', swap('gy', 1))  6.24 us
    ppermute x1, waiting for transfers between devices, shards(): lax.ppermute(total, 'gy', cross(step))  6.09 us
    pallas_call x1, Pallas kernels, shards(): pl.pallas_call(lambda *refs: sample_kernel(*refs, size=(size_x, size_y, s...  5.76 us
    ppermute x1, starting transfers between devices, shards(): far_x = lax.ppermute(faces[1], 'gx', swap('gx', 1))  5.68 us
    ppermute x3, starting transfers between devices, shards(): lax.ppermute(partial, 'gy', cross(step))  4.16 us
  transfers between devices with their start and end apart: 10, of which 4 were waited for; matrix products, arithmetic and copies ran while one was open for 0% of the time, Pallas kernels for 15%

profile of v1, /device:TPU:0, one launch (start us, length us, event | category | flops | bytes accessed | tf_op | source)
XLA Modules:
  0.0 75.7 jit_solution(1521509766189085941)
XLA Ops:
  0.6 0.0 copy-start.2
  0.7 2.1 %pack.1 = f32[32,24,128]{2,1,0:T(8,128)} custom-call(s32[16]{0:T(128)} %dest.1, s32[16,128]{1,0:T(8,128)} %bitcast.4, s32[16,128]{1,0:T(8,128)} %bitcast.6, f32[6,256]{1,0:T(8,128)} %motion.1, f32[3,2048]{1,0:T(4,128)} %offset.1, f32[8,2048]{1,0:T(8,128)} %refs_5_.1), custom_call_target="tpu_custom_call" | custom-call | tf_op jit(solution)/shard_map/pack/pallas_call | solution.py:496
  2.8 7.2 %all-to-all-start = ((f32[32,24,128]{2,1,0:T(8,128)}), f32[32,24,128]{2,1,0:T(8,128)S(1)}, u32[]{:S(2)}, u32[]{:S(2)}) async-start(f32[32,24,128]{2,1,0:T(8,128)} %pack.1), calls=%async_computation | async-start | bytes 786432 | tf_op jit(solution)/shard_map/all_to_all | solution.py:526
  10.0 0.6 moments.1
  10.6 0.1 pad_add_fusion.place.refs_0_
  10.7 13.2 %all-to-all-done.refs_0_.slots = f32[32,24,128]{2,1,0:T(8,128)S(1)} async-done(((f32[32,24,128]{2,1,0:T(8,128)}), f32[32,24,128]{2,1,0:T(8,128)S(1)}, u32[]{:S(2)}, u32[]{:S(2)}) %all-to-all-start) | async-done | bytes 393248 | tf_op jit(solution)/shard_map/all_to_all | solution.py:526
  23.9 5.8 %sample.1.pushed = f32[32,8,128]{2,1,0:T(8,128)} custom-call(f32[32,24,128]{2,1,0:T(8,128)S(1)} %all-to-all-done.refs_0_.slots, bf16[768,256]{1,0:T(8,128)(2,1)S(1)} %get-tuple-element.12.refs_1_), custom_call_target="tpu_custom_call" | custom-call | tf_op jit(solution)/shard_map/sample/pallas_call | solution.py:538
  29.7 3.9 %all-to-all-start.1 = ((f32[32,8,128]{2,1,0:T(8,128)}), f32[32,8,128]{2,1,0:T(8,128)S(1)}, u32[]{:S(2)}, u32[]{:S(2)}) async-start(f32[32,8,128]{2,1,0:T(8,128)} %sample.1.pushed), calls=%async_computation.1 | async-start | bytes 262144 | tf_op jit(solution)/shard_map/all_to_all | solution.py:546
  33.5 0.0 copy-start.1
  33.5 0.0 copy-start.3
  33.5 0.0 copy-start.7
  33.6 10.1 %spread.1 = (f32[19,4,32,128]{3,2,1,0:T(8,128)S(1)}, f32[5,32,128]{2,1,0:T(8,128)S(1)}, f32[5,32,128]{2,1,0:T(8,128)S(1)}, f32[24,128]{1,0:T(8,128)S(1)}, f32[24,128]{1,0:T(8,128)S(1)}) custom-call(s32[2]{0:T(128)S(1)} %pad_add_fusion.place.refs_0_, f32[32,24,128]{2,1,0:T(8,128)S(1)} %all-to-all-done.refs_0_.slots, f32[32,8,128]{2,1,0:T(8,128)} %sample.1.pushed, ...), custom_call_target="tpu_custom_call" | custom-call | flops 6000000000 | bytes 8000000 | tf_op jit(solution)/shard_map/spread/pallas_call | solution.py:548
  43.7 0.3 collective-permute-start
  44.0 5.7 %collective-permute-start.1 = (f32[5,32,128]{2,1,0:T(8,128)S(1)}, f32[5,32,128]{2,1,0:T(8,128)S(1)}, u32[]{:S(2)}, u32[]{:S(2)}) collective-permute-start(f32[5,32,128]{2,1,0:T(8,128)S(1)} %get-tuple-element.15), channel_id=1, source_target_pairs={{0,248},{8,16},{16,8},{24,32},{32,24},{40,48},{48,40},{56,64},{64,... | collective-permute-start | bytes 245768 | tf_op jit(solution)/shard_map/ppermute | solution.py:568
  49.7 0.0 all-to-all-done.1.returned
  49.7 1.0 %grain.1.refs_5_ = f32[8,256]{1,0:T(8,128)S(1)} custom-call(s32[16]{0:T(128)S(1)} %copy-done.7, s32[16,128]{1,0:T(8,128)S(1)} %bitcast.5, f32[3,2048]{1,0:T(4,128)S(1)} %copy-done.1, f32[32,8,128]{2,1,0:T(8,128)S(1)} %all-to-all-done.1.returned, f32[24,128]{1,0:T(8,128)S(1)} %get-tuple-element.16.after.refs_3_), custom_call_target="tpu_custom_call" | custom-call | tf_op jit(solution)/shard_map/grain/pallas_call | solution.py:570
  50.7 2.8 %collective-permute-start.4 = (f32[8,256]{1,0:T(8,128)S(1)}, f32[8,256]{1,0:T(8,128)S(1)}, u32[]{:S(2)}, u32[]{:S(2)}) collective-permute-start(f32[8,256]{1,0:T(8,128)S(1)} %grain.1.refs_5_), channel_id=1, source_target_pairs={{0,3},{1,2},{2,1},{3,0},{4,7},{5,6},{6,5},{7,4},{8,11},{9,10},{10,... | collective-permute-start | bytes 24584 | tf_op jit(solution)/shard_map/ppermute | solution.py:580
  53.6 0.8 %collective-permute-start.3 = (f32[8,256]{1,0:T(8,128)S(1)}, f32[8,256]{1,0:T(8,128)S(1)}, u32[]{:S(2)}, u32[]{:S(2)}) collective-permute-start(f32[8,256]{1,0:T(8,128)S(1)} %grain.1.refs_5_), channel_id=1, source_target_pairs={{0,2},{1,3},{2,0},{3,1},{4,6},{5,7},{6,4},{7,5},{8,10},{9,11},{10,... | collective-permute-start | bytes 24584 | tf_op jit(solution)/shard_map/ppermute | solution.py:580
  54.3 0.5 collective-permute-start.2
  54.9 0.0 collective-permute-done.refs_1_.near_x
  54.9 0.0 collective-permute-done.1.refs_2_.far_x
  54.9 0.8 %collective-permute-done.4.refs_8_ = f32[8,256]{1,0:T(8,128)S(1)} collective-permute-done((f32[8,256]{1,0:T(8,128)S(1)}, f32[8,256]{1,0:T(8,128)S(1)}, u32[]{:S(2)}, u32[]{:S(2)}) %collective-permute-start.4) | collective-permute-done | bytes 8224 | tf_op jit(solution)/shard_map/ppermute | solution.py:580
  55.7 3.1 %collective-permute-done.3.refs_7_ = f32[8,256]{1,0:T(8,128)S(1)} collective-permute-done((f32[8,256]{1,0:T(8,128)S(1)}, f32[8,256]{1,0:T(8,128)S(1)}, u32[]{:S(2)}, u32[]{:S(2)}) %collective-permute-start.3) | collective-permute-done | bytes 8224 | tf_op jit(solution)/shard_map/ppermute | solution.py:580
  58.7 0.0 collective-permute-done.2.refs_6_
  58.7 0.6 edge.1
  59.3 0.3 collective-permute-start.5
  59.6 6.2 %collective-permute-start.6 = (f32[24,128]{1,0:T(8,128)S(1)}, f32[24,128]{1,0:T(8,128)S(1)}, u32[]{:S(2)}, u32[]{:S(2)}) collective-permute-start(f32[24,128]{1,0:T(8,128)S(1)} %get-tuple-element.19), channel_id=1, source_target_pairs={{0,7},{1,2},{2,1},{3,4},{4,3},{5,6},{6,5},{7,0},{8,15},{9,10},{10,... | collective-permute-start | bytes 36872 | tf_op jit(solution)/shard_map/ppermute | solution.py:591
  65.9 1.5 %collective-permute-start.7 = (f32[8,256]{1,0:T(8,128)S(1)}, f32[8,256]{1,0:T(8,128)S(1)}, u32[]{:S(2)}, u32[]{:S(2)}) collective-permute-start(f32[8,256]{1,0:T(8,128)S(1)} %get-tuple-element.21.refs_1_), channel_id=1, source_target_pairs={{0,4},{1,5},{2,6},{3,7},{4,0},{5,1},{6,2},{7,3},{8,12},{9,13},{10,... | collective-permute-start | bytes 24584 | tf_op jit(solution)/shard_map/ppermute | solution.py:592
  67.3 6.1 %collective-permute-done.7.refs_2_ = f32[8,256]{1,0:T(8,128)S(1)} collective-permute-done((f32[8,256]{1,0:T(8,128)S(1)}, f32[8,256]{1,0:T(8,128)S(1)}, u32[]{:S(2)}, u32[]{:S(2)}) %collective-permute-start.7) | collective-permute-done | bytes 8224 | tf_op jit(solution)/shard_map/ppermute | solution.py:592
  73.4 0.0 collective-permute-done.5.near_y
  73.4 0.0 collective-permute-done.6.far_y
  73.4 2.3 %stream.1 = (f32[19,4,32,128]{3,2,1,0:T(8,128)}, f32[6,256]{1,0:T(8,128)}) custom-call(s32[2]{0:T(128)S(1)} %pad_add_fusion.place.refs_0_, f32[19,4,32,128]{3,2,1,0:T(8,128)S(1)} %get-tuple-element.13.collided, f32[5,32,128]{2,1,0:T(8,128)S(1)} %collective-permute-done.refs_1_.near_x, f32[5,32,128]{2,1,0:T(8,128)S(1)} %collective-permute-done.1.refs_2_.far_x, ...), custom_call_target="tpu_custom_call" | custom-call | tf_op jit(solution)/shard_map/stream/pallas_call | solution.py:594
  (12 shorter events, 0.0 us)
Async XLA Ops:
  0.6 9.4 %copy-start.2 = (f32[6,256]{1,0:T(8,128)S(1)}, f32[6,256]{1,0:T(8,128)}, u32[]{:S(2)}) copy-start(f32[6,256]{1,0:T(8,128)} %motion.1) | copy-start | bytes 18436
  0.6 9.4 %copy-start = (f32[19,4,32,128]{3,2,1,0:T(8,128)S(1)}, f32[19,4,32,128]{3,2,1,0:T(8,128)}, u32[]{:S(2)}) copy-start(f32[19,4,32,128]{3,2,1,0:T(8,128)} %populations.3) | copy-start | bytes 3735556
  0.7 9.4 %copy-start.4 = (f32[3,512]{1,0:T(4,128)S(1)}, f32[3,512]{1,0:T(4,128)}, u32[]{:S(2)}) copy-start(f32[3,512]{1,0:T(4,128)} %rest.1) | copy-start | bytes 18436
  0.7 9.4 %copy-start.5 = (s32[2,512]{1,0:T(2,128)S(1)}, s32[2,512]{1,0:T(2,128)}, u32[]{:S(2)}) copy-start(s32[2,512]{1,0:T(2,128)} %pairs.1) | copy-start | bytes 12292
  0.7 9.4 %copy-start.6 = (f32[3,256]{1,0:T(4,128)S(1)}, f32[3,256]{1,0:T(4,128)}, u32[]{:S(2)}) copy-start(f32[3,256]{1,0:T(4,128)} %position.1) | copy-start | bytes 9220
  2.8 21.1 %all-to-all-start = ((f32[32,24,128]{2,1,0:T(8,128)}), f32[32,24,128]{2,1,0:T(8,128)S(1)}, u32[]{:S(2)}, u32[]{:S(2)}) async-start(f32[32,24,128]{2,1,0:T(8,128)} %pack.1), calls=%async_computation | async-start | bytes 786432 | tf_op jit(solution)/shard_map/all_to_all | solution.py:526
  29.7 20.0 %all-to-all-start.1 = ((f32[32,8,128]{2,1,0:T(8,128)}), f32[32,8,128]{2,1,0:T(8,128)S(1)}, u32[]{:S(2)}, u32[]{:S(2)}) async-start(f32[32,8,128]{2,1,0:T(8,128)} %sample.1.pushed), calls=%async_computation.1 | async-start | bytes 262144 | tf_op jit(solution)/shard_map/all_to_all | solution.py:546
  33.5 16.1 %copy-start.1 = (f32[3,2048]{1,0:T(4,128)S(1)}, f32[3,2048]{1,0:T(4,128)}, u32[]{:S(2)}) copy-start(f32[3,2048]{1,0:T(4,128)} %offset.1) | copy-start | bytes 73732
  33.5 16.1 %copy-start.3 = (s32[2048]{0:T(1024)S(1)}, s32[2048]{0:T(1024)}, u32[]{:S(2)}) copy-start(s32[2048]{0:T(1024)} %param.13) | copy-start | bytes 24580
  33.5 16.1 %copy-start.7 = (s32[16]{0:T(128)S(1)}, s32[16]{0:T(128)}, u32[]{:S(2)}) copy-start(s32[16]{0:T(128)} %dest.1) | copy-start | bytes 196
  43.7 11.2 %collective-permute-start = (f32[5,32,128]{2,1,0:T(8,128)S(1)}, f32[5,32,128]{2,1,0:T(8,128)S(1)}, u32[]{:S(2)}, u32[]{:S(2)}) collective-permute-start(f32[5,32,128]{2,1,0:T(8,128)S(1)} %get-tuple-element.14), channel_id=1, source_target_pairs={{0,8},{8,0},{16,24},{24,16},{32,40},{40,32},{48,56},{56,48},{64,72... | collective-permute-start | bytes 245768 | tf_op jit(solution)/shard_map/ppermute | solution.py:567
  44.0 10.9 %collective-permute-start.1 = (f32[5,32,128]{2,1,0:T(8,128)S(1)}, f32[5,32,128]{2,1,0:T(8,128)S(1)}, u32[]{:S(2)}, u32[]{:S(2)}) collective-permute-start(f32[5,32,128]{2,1,0:T(8,128)S(1)} %get-tuple-element.15), channel_id=1, source_target_pairs={{0,248},{8,16},{16,8},{24,32},{32,24},{40,48},{48,40},{56,64},{64,... | collective-permute-start | bytes 245768 | tf_op jit(solution)/shard_map/ppermute | solution.py:568
  50.7 4.9 %collective-permute-start.4 = (f32[8,256]{1,0:T(8,128)S(1)}, f32[8,256]{1,0:T(8,128)S(1)}, u32[]{:S(2)}, u32[]{:S(2)}) collective-permute-start(f32[8,256]{1,0:T(8,128)S(1)} %grain.1.refs_5_), channel_id=1, source_target_pairs={{0,3},{1,2},{2,1},{3,0},{4,7},{5,6},{6,5},{7,4},{8,11},{9,10},{10,... | collective-permute-start | bytes 24584 | tf_op jit(solution)/shard_map/ppermute | solution.py:580
  53.6 5.2 %collective-permute-start.3 = (f32[8,256]{1,0:T(8,128)S(1)}, f32[8,256]{1,0:T(8,128)S(1)}, u32[]{:S(2)}, u32[]{:S(2)}) collective-permute-start(f32[8,256]{1,0:T(8,128)S(1)} %grain.1.refs_5_), channel_id=1, source_target_pairs={{0,2},{1,3},{2,0},{3,1},{4,6},{5,7},{6,4},{7,5},{8,10},{9,11},{10,... | collective-permute-start | bytes 24584 | tf_op jit(solution)/shard_map/ppermute | solution.py:580
  54.3 4.4 %collective-permute-start.2 = (f32[8,256]{1,0:T(8,128)S(1)}, f32[8,256]{1,0:T(8,128)S(1)}, u32[]{:S(2)}, u32[]{:S(2)}) collective-permute-start(f32[8,256]{1,0:T(8,128)S(1)} %grain.1.refs_5_), channel_id=1, source_target_pairs={{0,1},{1,0},{2,3},{3,2},{4,5},{5,4},{6,7},{7,6},{8,9},{9,8},{10,11... | collective-permute-start | bytes 24584 | tf_op jit(solution)/shard_map/ppermute | solution.py:580
  59.3 14.1 %collective-permute-start.5 = (f32[24,128]{1,0:T(8,128)S(1)}, f32[24,128]{1,0:T(8,128)S(1)}, u32[]{:S(2)}, u32[]{:S(2)}) collective-permute-start(f32[24,128]{1,0:T(8,128)S(1)} %get-tuple-element.18), channel_id=1, source_target_pairs={{0,1},{1,0},{2,3},{3,2},{4,5},{5,4},{6,7},{7,6},{8,9},{9,8},{10,11... | collective-permute-start | bytes 36872 | tf_op jit(solution)/shard_map/ppermute | solution.py:590
  59.6 13.8 %collective-permute-start.6 = (f32[24,128]{1,0:T(8,128)S(1)}, f32[24,128]{1,0:T(8,128)S(1)}, u32[]{:S(2)}, u32[]{:S(2)}) collective-permute-start(f32[24,128]{1,0:T(8,128)S(1)} %get-tuple-element.19), channel_id=1, source_target_pairs={{0,7},{1,2},{2,1},{3,4},{4,3},{5,6},{6,5},{7,0},{8,15},{9,10},{10,... | collective-permute-start | bytes 36872 | tf_op jit(solution)/shard_map/ppermute | solution.py:591
  65.9 7.6 %collective-permute-start.7 = (f32[8,256]{1,0:T(8,128)S(1)}, f32[8,256]{1,0:T(8,128)S(1)}, u32[]{:S(2)}, u32[]{:S(2)}) collective-permute-start(f32[8,256]{1,0:T(8,128)S(1)} %get-tuple-element.21.refs_1_), channel_id=1, source_target_pairs={{0,4},{1,5},{2,6},{3,7},{4,0},{5,1},{6,2},{7,3},{8,12},{9,13},{10,... | collective-permute-start | bytes 24584 | tf_op jit(solution)/shard_map/ppermute | solution.py:592

commit v2 on v1

--- a/solution.py
+++ b/solution.py
@@ -10,8 +10,11 @@
 SLOT_ROWS = 24
 BACK_ROWS = 8
 EDGE_ROWS = 24
-UNROLL = 8
-REDUCE_STEPS = ((1, 2, 3), (4,))
+SAMPLE_GROUP = 2
+SAMPLE_UNROLL = 16
+SPREAD_GROUP = 8
+SPREAD_UNROLL = 4
+CHUNK = 8
 
 
 LATTICE = (
@@ -50,7 +53,6 @@
 VMEM = pl.BlockSpec(memory_space=pltpu.VMEM)
 SMEM = pl.BlockSpec(memory_space=pltpu.SMEM)
 HBM = pl.BlockSpec(memory_space=pltpu.HBM)
-ANYWHERE = pl.BlockSpec(memory_space=pl.ANY)
 F32 = jnp.float32
 BF16 = jnp.bfloat16
 
@@ -202,56 +204,79 @@
     bond_part(pairs, rest, position, motion, bonded)
 
 
-def marker_tables(slots, size_x, size_y, size_z):
+def marker_places(slots, size_x, size_y, size_z):
     cells = jnp.concatenate([slots[19:20], slots[23:24]], axis=1).astype(jnp.int32)
     weight = jnp.concatenate([slots[0:8], slots[8:16]], axis=1)
     place_x = lax.shift_right_logical(cells, (size_y * size_z).bit_length() - 1)
     place_y = lax.shift_right_logical(cells, size_z.bit_length() - 1) & (size_y - 1)
     place_z = cells & (size_z - 1)
-    depth = one_hot(size_z, place_z)
-    row = lax.broadcasted_iota(jnp.int32, (size_y, cells.shape[1]), 0)
+    shares = []
+    for x in range(size_x):
+        share = jnp.where(place_x == x - 1, weight[4:8], 0.0)
+        shares.append(jnp.where(place_x == x, weight[0:4], share))
+    return shares, place_y, one_hot(size_z, place_z)
+
+
+def marker_shares(shares, place_y, size_y):
+    row = lax.broadcasted_iota(jnp.int32, (size_y, place_y.shape[1]), 0)
     at_low = row == place_y
     at_high = row == place_y + 1
-    shares = [[None] * size_x, [None] * size_x]
-    for x in range(size_x):
-        share = jnp.where(place_x == x - 1, weight[4:8], 0.0)
-        share = jnp.where(place_x == x, weight[0:4], share)
-        for step in range(2):
-            value = jnp.where(at_high, share[2 + step : 3 + step], 0.0)
-            shares[step][x] = jnp.where(at_low, share[step : step + 1], value)
-    return depth, shares
+    tables = [[], []]
+    for share in shares:
+        for corner in range(2):
+            value = jnp.where(at_high, share[2 + corner : 3 + corner], 0.0)
+            tables[corner].append(jnp.where(at_low, share[corner : corner + 1], value))
+    return tables
+
+
+def marker_halves(shares, place_y, size_y):
+    at_low = one_hot(size_y, place_y)
+    at_high = one_hot(size_y, place_y + 1)
+    tables = [[], []]
+    for part in range(2):
+        split = [halves(share)[part] for share in shares]
+        for corner in range(2):
+            for share in split:
+                low = at_low * share[corner : corner + 1]
+                high = at_high * share[2 + corner : 3 + corner]
+                tables[part].append(low + high)
+    return [jnp.concatenate(table, axis=0) for table in tables]
 
 
 def sample_kernel(slots, table, pushed, *, size):
     size_x, size_y, size_z = size
     planes = size_x * size_y
 
-    def body(source, carry):
-        rows = slots[source]
-        depth, shares = marker_tables(rows, size_x, size_y, size_z)
-        found = lax.dot_general(
-            table[...],
-            jnp.concatenate([depth, depth], axis=0),
-            NN,
-            preferred_element_type=F32,
-        )
-        target = jnp.concatenate([rows[16:19], rows[20:23]], axis=1)
-        force = []
-        for axis in range(3):
-            value = None
-            for step in range(2):
-                for x in range(size_x):
-                    first = (step * 3 + axis) * planes + x * size_y
-                    term = shares[step][x] * found[first : first + size_y]
-                    value = term if value is None else value + term
-            sampled = jnp.sum(value, axis=0, keepdims=True)
-            force.append(STIFFNESS * (target[axis : axis + 1] - sampled))
-        blank = jnp.zeros_like(force[0])
-        force = jnp.concatenate(force + [blank], axis=0)
-        pushed[source] = jnp.concatenate([force[:, :MARKS], force[:, MARKS:]], axis=0)
+    def body(step, carry):
+        tables = []
+        for part in range(SAMPLE_GROUP):
+            rows = slots[step * SAMPLE_GROUP + part]
+            shares, place_y, depth = marker_places(rows, size_x, size_y, size_z)
+            tables.append((rows, depth, marker_shares(shares, place_y, size_y)))
+        depth = jnp.concatenate([entry[1] for entry in tables], axis=1)
+        depth = jnp.concatenate([depth, depth], axis=0)
+        found = lax.dot_general(table[...], depth, NN, preferred_element_type=F32)
+        for part, (rows, _, shares) in enumerate(tables):
+            span = slice(part * 2 * MARKS, (part + 1) * 2 * MARKS)
+            target = jnp.concatenate([rows[16:19], rows[20:23]], axis=1)
+            force = []
+            for axis in range(3):
+                value = None
+                for corner in range(2):
+                    for x in range(size_x):
+                        first = (corner * 3 + axis) * planes + x * size_y
+                        term = shares[corner][x] * found[first : first + size_y, span]
+                        value = term if value is None else value + term
+                sampled = jnp.sum(value, axis=0, keepdims=True)
+                force.append(STIFFNESS * (target[axis : axis + 1] - sampled))
+            blank = jnp.zeros_like(force[0])
+            force = jnp.concatenate(force + [blank], axis=0)
+            pushed[step * SAMPLE_GROUP + part] = jnp.concatenate(
+                [force[:, :MARKS], force[:, MARKS:]], axis=0
+            )
         return carry
 
-    lax.fori_loop(0, slots.shape[0], body, 0, unroll=UNROLL)
+    lax.fori_loop(0, slots.shape[0] // SAMPLE_GROUP, body, 0, unroll=SAMPLE_UNROLL)
 
 
 def spread_kernel(
@@ -261,98 +286,91 @@
     planes = size_x * size_y
     total[...] = jnp.zeros_like(total)
 
-    def body(source, carry):
-        depth, shares = marker_tables(slots[source], size_x, size_y, size_z)
-        both = pushed[source]
-        force = jnp.concatenate([both[0:4], both[4:8]], axis=1)
-        high = []
-        low = []
-        for step in range(2):
-            for axis in range(3):
-                for x in range(size_x):
-                    one, two = halves(MARKER_AREA * force[axis : axis + 1] * shares[step][x])
-                    high.append(one)
-                    low.append(two)
-        left = jnp.concatenate(
-            [jnp.concatenate(high, axis=0), jnp.concatenate(low, axis=0)], axis=1
+    def body(step, carry):
+        wide, thin, strong, weak = [], [], [], []
+        for part in range(SPREAD_GROUP):
+            source = step * SPREAD_GROUP + part
+            shares, place_y, depth = marker_places(slots[source], size_x, size_y, size_z)
+            first, second = marker_halves(shares, place_y, size_y)
+            both = pushed[source]
+            force = MARKER_AREA * jnp.concatenate([both[0:4], both[4:8]], axis=1)
+            high, low = halves(force)
+            wide.append(first)
+            thin.append(second)
+            strong.append(jnp.concatenate([depth * high[a : a + 1] for a in range(3)], axis=0))
+            weak.append(jnp.concatenate([depth * low[a : a + 1] for a in range(3)], axis=0))
+        wide, thin, strong, weak = (
+            jnp.concatenate(part, axis=1) for part in (wide, thin, strong, weak)
         )
-        right = jnp.concatenate([depth, depth], axis=1)
-        total[...] += lax.dot_general(left, right, NT, preferred_element_type=F32)
+        most = lax.dot_general(
+            jnp.concatenate([strong, weak], axis=0), wide, NT, preferred_element_type=F32
+        )
+        rest = lax.dot_general(strong, thin, NT, preferred_element_type=F32)
+        height = strong.shape[0]
+        total[...] += most[:height] + (most[height:] + rest)
         return carry
 
-    lax.fori_loop(0, slots.shape[0], body, 0, unroll=UNROLL)
+    lax.fori_loop(0, slots.shape[0] // SPREAD_GROUP, body, 0, unroll=SPREAD_UNROLL)
+
+    for axis in range(3):
+        span = slice(axis * size_z, (axis + 1) * size_z)
+        both = total[span, :planes] + pltpu.roll(total[span, planes:], 1, 0)
+        total[span, :planes] = both.T
 
     factor = 1.0 - 0.5 / RELAX_TIME
     for x in range(size_x):
-        current = [populations[q, x] for q in range(quantity)]
-        density = sum_of(current)
-        inverse = 1.0 / density
-        momentum = momentum_of(current)
-        forcing = []
-        for axis in range(3):
-            first = axis * planes + x * size_y
-            near = total[first : first + size_y]
-            far = total[3 * planes + first : 3 * planes + first + size_y]
-            forcing.append(near + pltpu.roll(far, 1, 1))
-        velocity = [(momentum[a] + 0.5 * forcing[a]) * inverse for a in range(3)]
-        speed_square = sum_of([v * v for v in velocity])
-        flow_force = sum_of([velocity[a] * forcing[a] for a in range(3)])
-        rest_flow = 1.0 - 1.5 * speed_square
-        rest_force = -3.0 * flow_force
-        for number, vector in enumerate(LATTICE):
-            weight = lattice_weight(vector)
-            flow = rest_flow
-            push = rest_force
-            if any(vector):
-                along_flow = project(vector, velocity)
-                along_force = project(vector, forcing)
-                flow = flow + along_flow * (3.0 + 4.5 * along_flow)
-                push = push + along_force * (3.0 + 9.0 * along_flow)
-            value = (
-                (1.0 - 1.0 / RELAX_TIME) * current[number]
-                + (weight / RELAX_TIME) * density * flow
-                + (factor * weight) * push
-            )
-            collided[number, x] = value
-            if x == size_x - 1 and number in UP_X:
-                put_face(place[0] == 0, near_x, far_x, UP_X.index(number), value)
-            if x == 0 and number in DOWN_X:
-                put_face(place[0] == 1, near_x, far_x, DOWN_X.index(number), value)
-            if number in UP_Y:
-                line = UP_Y.index(number) * size_x + x
-                put_row(place[1] == 0, near_y, far_y, line, value[size_y - 1 : size_y])
-            if number in DOWN_Y:
-                line = DOWN_Y.index(number) * size_x + x
-                put_row(place[1] == 1, near_y, far_y, line, value[0:1])
+        for y in range(0, size_y, CHUNK):
+            rows = slice(y, y + CHUNK)
+            current = [populations[q, x, rows] for q in range(quantity)]
+            density = sum_of(current)
+            inverse = 1.0 / density
+            momentum = momentum_of(current)
+            forcing = []
+            for axis in range(3):
+                first = axis * size_z + x * size_y + y
+                forcing.append(total[first : first + CHUNK, :size_z])
+            velocity = [(momentum[a] + 0.5 * forcing[a]) * inverse for a in range(3)]
+            speed_square = sum_of([v * v for v in velocity])
+            flow_force = sum_of([velocity[a] * forcing[a] for a in range(3)])
+            rest_flow = 1.0 - 1.5 * speed_square
+            rest_force = -3.0 * flow_force
+            for number, vector in enumerate(LATTICE):
+                weight = lattice_weight(vector)
+                flow = rest_flow
+                push = rest_force
+                if any(vector):
+                    along_flow = project(vector, velocity)
+                    along_force = project(vector, forcing)
+                    flow = flow + along_flow * (3.0 + 4.5 * along_flow)
+                    push = push + along_force * (3.0 + 9.0 * along_flow)
+                collided[number, x, rows] = (
+                    (1.0 - 1.0 / RELAX_TIME) * current[number]
+                    + (weight / RELAX_TIME) * density * flow
+                    + (factor * weight) * push
+                )
+
+    even_x = place[0] == 0
+    for index, (up, down) in enumerate(zip(UP_X, DOWN_X)):
+        top = collided[up, size_x - 1]
+        bottom = collided[down, 0]
+        near_x[index] = jnp.where(even_x, top, bottom)
+        far_x[index] = jnp.where(even_x, bottom, top)
+    even_y = place[1] == 0
+    for index, (up, down) in enumerate(zip(UP_Y, DOWN_Y)):
+        for x in range(size_x):
+            top = collided[up, x, size_y - 1 : size_y]
+            bottom = collided[down, x, 0:1]
+            line = index * size_x + x
+            near_y[line : line + 1] = jnp.where(even_y, top, bottom)
+            far_y[line : line + 1] = jnp.where(even_y, bottom, top)
     filled = len(UP_Y) * size_x
     for face in (near_y, far_y):
         face[filled:] = jnp.zeros_like(face[filled:])
 
 
-def put_face(to_near, near, far, index, value):
-    @pl.when(to_near)
-    def _():
-        near[index] = value
-
-    @pl.when(jnp.logical_not(to_near))
-    def _():
-        far[index] = value
-
-
-def put_row(to_near, near, far, line, value):
-    @pl.when(to_near)
-    def _():
-        near[line : line + 1] = value
-
-    @pl.when(jnp.logical_not(to_near))
-    def _():
-        far[line : line + 1] = value
-
-
 def edge_kernel(
-    place, near_x, far_x, near_y, far_y, *refs, size_x
+    place, near_x, far_x, near_y, far_y, partial, near_out, far_out, *, size_x
 ):
-    parts, (near_out, far_out, total_out) = refs[:-3], refs[-3:]
     size_y = near_x.shape[1]
     filled = len(UP_Y) * size_x
     even_x = place[0] == 0
@@ -366,11 +384,22 @@
     up = jnp.concatenate([from_x(LATTICE.index((1, 1, 0)), top), to_x(LATTICE.index((-1, 1, 0)), top)], axis=0)
     down = jnp.concatenate([from_x(LATTICE.index((1, -1, 0)), 0), to_x(LATTICE.index((-1, -1, 0)), 0)], axis=0)
     even_y = place[1] == 0
-    near_out[...] = near_y[...]
+    near_out[:EDGE_ROWS] = near_y[...]
     far_out[...] = far_y[...]
+    width = near_out.shape[1]
+    for part in range(partial.shape[1] // width):
+        first = EDGE_ROWS + 8 * part
+        near_out[first : first + 8] = partial[:, part * width : (part + 1) * width]
     near_out[filled : filled + 2] = jnp.where(even_y, up, down)
     far_out[filled : filled + 2] = jnp.where(even_y, down, up)
-    total_out[...] = sum_of([part[...] for part in parts])
+
+
+def pair_kernel(partial, near_y, total):
+    width = near_y.shape[1]
+    for part in range(partial.shape[1] // width):
+        first = EDGE_ROWS + 8 * part
+        span = slice(part * width, (part + 1) * width)
+        total[:, span] = partial[:, span] + near_y[first : first + 8]
 
 
 def project(vector, field):
@@ -387,24 +416,15 @@
     return value
 
 
-def stream_kernel(
-    place, collided, near_x, far_x, near_y, far_y, *refs
-):
-    parts, (out, load, stage, sems) = refs[:-4], refs[-4:]
+def stream_kernel(place, collided, near_x, far_x, out, strips, stage, sems):
     quantity, size_x, size_y, size_z = collided.shape
-    row = lax.broadcasted_iota(jnp.int32, (size_y, size_z), 0)
     lane = lax.broadcasted_iota(jnp.int32, (size_y, size_z), 1)
     even_x = place[0] == 0
-    even_y = place[1] == 0
-    filled = len(UP_Y) * size_x
-    from_y = jnp.where(even_y, far_y[...], near_y[...])
-    to_y = jnp.where(even_y, near_y[...], far_y[...])
     copies = []
     for x in (1, 2, 0, 3):
         for number, vector in enumerate(LATTICE):
             source = x - vector[0]
-            inside = 0 <= source < size_x
-            if inside:
+            if 0 <= source < size_x:
                 value = collided[number, source]
             elif vector[0] == 1:
                 index = UP_X.index(number)
@@ -413,17 +433,7 @@
                 index = DOWN_X.index(number)
                 value = jnp.where(even_x, near_x[index], far_x[index])
             if vector[1]:
-                face = from_y if vector[1] == 1 else to_y
-                column = UP_Y if vector[1] == 1 else DOWN_Y
-                if inside:
-                    line = column.index(number) * size_x + source
-                else:
-                    line = filled if vector[0] == 1 else filled + 1
-                ghost = face[line : line + 1]
-                if vector[1] == 1:
-                    value = jnp.where(row == 0, ghost, pltpu.roll(value, 1, 0))
-                else:
-                    value = jnp.where(row == size_y - 1, ghost, pltpu.roll(value, size_y - 1, 0))
+                value = pltpu.roll(value, 1 if vector[1] == 1 else size_y - 1, 0)
             if vector[2]:
                 back = collided[OPPOSITE[number], x]
                 if vector[2] == 1:
@@ -431,9 +441,51 @@
                 else:
                     value = jnp.where(lane == size_z - 1, back, pltpu.roll(value, size_z - 1, 1))
             stage[number, x] = value
+            if vector[1] == 1:
+                strips[UP_Y.index(number), x] = value[:8]
+            elif vector[1] == -1:
+                strips[len(UP_Y) + DOWN_Y.index(number), x] = value[size_y - 8 :]
         copy = pltpu.make_async_copy(stage.at[:, x], out.at[:, x], sems.at[x])
         copy.start()
         copies.append(copy)
+    for copy in copies:
+        copy.wait()
+
+
+def rim_kernel(place, strips, near_y, far_y, *refs):
+    parts, (given, out, load, stage, sems) = refs[:-5], refs[-5:]
+    size_x, size_y, size_z = out.shape[1:]
+    row = lax.broadcasted_iota(jnp.int32, (8, size_z), 0)
+    lane = lax.broadcasted_iota(jnp.int32, (8, size_z), 1)
+    even_y = place[1] == 0
+    filled = len(UP_Y) * size_x
+    near, far = near_y[:EDGE_ROWS], far_y[...]
+    from_y = jnp.where(even_y, far, near)
+    to_y = jnp.where(even_y, near, far)
+    copies = []
+    for group, (face, column, edge) in enumerate(((from_y, UP_Y, 0), (to_y, DOWN_Y, 7))):
+        for index, number in enumerate(column):
+            vector = LATTICE[number]
+            slot = group * len(UP_Y) + index
+            for x in range(size_x):
+                source = x - vector[0]
+                if 0 <= source < size_x:
+                    line = index * size_x + source
+                else:
+                    line = filled if vector[0] == 1 else filled + 1
+                ghost = jnp.broadcast_to(face[line : line + 1], (8, size_z))
+                replace = row == edge
+                if vector[2] == 1:
+                    ghost = pltpu.roll(ghost, 1, 1)
+                    replace = jnp.logical_and(replace, lane != 0)
+                elif vector[2] == -1:
+                    ghost = pltpu.roll(ghost, size_z - 1, 1)
+                    replace = jnp.logical_and(replace, lane != size_z - 1)
+                stage[slot, x] = jnp.where(replace, ghost, strips[slot, x])
+            rows = pl.ds(0 if edge == 0 else size_y - 8, 8)
+            copy = pltpu.make_async_copy(stage.at[slot], out.at[number, :, rows], sems.at[slot])
+            copy.start()
+            copies.append(copy)
     total = sum_of([part[...] for part in parts])
     load[...] = total[: load.shape[0]]
     for copy in copies:
@@ -556,7 +608,7 @@
         ],
         in_specs=[SMEM] + [VMEM] * 3,
         out_specs=[VMEM] * 5,
-        scratch_shapes=[pltpu.VMEM((6 * planes, size_z), F32)],
+        scratch_shapes=[pltpu.VMEM((3 * size_z, 2 * planes), F32)],
         compiler_params=params,
         cost_estimate=pl.CostEstimate(
             flops=6000000000, bytes_accessed=8000000, transcendentals=0
@@ -564,45 +616,71 @@
         name="spread",
     )(place, slots, pushed, populations)
 
-    near_x = lax.ppermute(faces[0], "gx", swap("gx", 0))
-    far_x = lax.ppermute(faces[1], "gx", swap("gx", 1))
-
     partial = pl.pallas_call(
         grain_kernel,
         out_shape=shape((8, slab), F32),
-        in_specs=[SMEM] + [VMEM] * 3 + [ANYWHERE],
+        in_specs=[SMEM] + [VMEM] * 3 + [HBM],
         out_specs=VMEM,
         scratch_shapes=[pltpu.SMEM((bricks,), jnp.int32)],
         compiler_params=params,
         name="grain",
     )(block_dest, grain_blocks, marker_offset, returned, faces[2])
-    first, second = REDUCE_STEPS
-    parts = [partial] + [lax.ppermute(partial, "gy", cross(step)) for step in first]
-
-    near_y, far_y, total = pl.pallas_call(
+    near_x = lax.ppermute(faces[0], "gx", swap("gx", 0))
+    far_x = lax.ppermute(faces[1], "gx", swap("gx", 1))
+    near_y, far_y = pl.pallas_call(
         lambda *refs: edge_kernel(*refs, size_x=size_x),
-        out_shape=[shape((EDGE_ROWS, size_z), F32)] * 2 + [shape((8, slab), F32)],
-        in_specs=[SMEM] + [VMEM] * (4 + len(parts)),
-        out_specs=[VMEM] * 3,
+        out_shape=[
+            shape((EDGE_ROWS + 8 * slab // size_z, size_z), F32),
+            shape((EDGE_ROWS, size_z), F32),
+        ],
+        in_specs=[SMEM] + [VMEM] * 5,
+        out_specs=[VMEM] * 2,
         compiler_params=params,
         name="edge",
-    )(place, near_x, far_x, faces[2], faces[3], *parts)
+    )(place, near_x, far_x, faces[2], faces[3], partial)
     near_y = lax.ppermute(near_y, "gy", swap("gy", 0))
     far_y = lax.ppermute(far_y, "gy", swap("gy", 1))
-    parts = [bonded, total] + [lax.ppermute(total, "gy", cross(step)) for step in second]
-
-    populations_next, grain_load = pl.pallas_call(
+    total = pl.pallas_call(
+        pair_kernel,
+        out_shape=shape((8, slab), F32),
+        in_specs=[VMEM] * 2,
+        out_specs=VMEM,
+        compiler_params=params,
+        name="pair",
+    )(partial, near_y)
+    parts = [bonded, total]
+    parts += [lax.ppermute(total, "gy", cross(step)) for step in range(2, lax.axis_size("gy"), 2)]
+
+    streamed, strips = pl.pallas_call(
         stream_kernel,
-        out_shape=[shape(populations.shape, F32), shape((6, slab), F32)],
-        in_specs=[SMEM] + [VMEM] * (5 + len(parts)),
-        out_specs=[ANYWHERE, VMEM],
+        out_shape=[
+            shape(populations.shape, F32),
+            shape((len(UP_Y) + len(DOWN_Y), size_x, 8, size_z), F32),
+        ],
+        in_specs=[SMEM] + [VMEM] * 3,
+        out_specs=[HBM, VMEM],
         scratch_shapes=[
             pltpu.VMEM(populations.shape, F32),
             pltpu.SemaphoreType.DMA((size_x,)),
         ],
         compiler_params=params,
+        cost_estimate=pl.CostEstimate(flops=20000000, bytes_accessed=4000000, transcendentals=0),
         name="stream",
-    )(place, collided, near_x, far_x, near_y, far_y, *parts)
+    )(place, collided, near_x, far_x)
+
+    populations_next, grain_load = pl.pallas_call(
+        rim_kernel,
+        out_shape=[shape(populations.shape, F32), shape((6, slab), F32)],
+        in_specs=[SMEM] + [VMEM] * (3 + len(parts)) + [HBM],
+        out_specs=[HBM, VMEM],
+        scratch_shapes=[
+            pltpu.VMEM(strips.shape, F32),
+            pltpu.SemaphoreType.DMA((strips.shape[0],)),
+        ],
+        input_output_aliases={4 + len(parts): 0},
+        compiler_params=params,
+        name="rim",
+    )(place, strips, near_y, far_y, *parts, streamed)
     return populations_next, grain_load
 
 

time: 76 us -> 71.8 us (0.945)
  the two profiles are of different devices: /device:TPU:0 before, /device:TPU:4 now
where the time goes in v2:
time: 71.8 us; the launch traced here: 71.5 us
  starting transfers between devices  29.7 us (41%)
  waiting for transfers between devices  20.5 us (29%)
  Pallas kernels  20.1 us (28%)
  between operations  0.99 us (1%)
    all_to_all x1, waiting for transfers between devices, shards(): lax.all_to_all(outgoing, 'gx', split_axis=0, concat_axis=0, tiled=True)  13.2 us
    ppermute x3, starting transfers between devices, shards(): lax.ppermute(total, 'gy', cross(step))  9.65 us
    all_to_all x1, starting transfers between devices, shards(): lax.all_to_all(outgoing, 'gx', split_axis=0, concat_axis=0, tiled=True)  8.93 us
    pallas_call x1, Pallas kernels, shards(): pl.pallas_call(spread_kernel, out_shape=[shape(populations.shape, F32), s...  6.87 us
    ppermute x1, starting transfers between devices, shards(): far_x = lax.ppermute(faces[1], 'gx', swap('gx', 1))  5.54 us
    pallas_call x1, Pallas kernels, shards(): pl.pallas_call(lambda *refs: sample_kernel(*refs, size=(size_x, size_y, s...  5.34 us
    all_to_all x1, starting transfers between devices, shards(): lax.all_to_all(pushed, 'gx', split_axis=0, concat_axis=0, tiled=True)  4.04 us
    ppermute x3, waiting for transfers between devices, shards(): lax.ppermute(total, 'gy', cross(step))  3.42 us
  transfers between devices with their start and end apart: 9, of which 5 were waited for; matrix products, arithmetic and copies ran while one was open for 0% of the time, Pallas kernels for 14%

profile of v2, /device:TPU:4, one launch (start us, length us, event | category | flops | bytes accessed | tf_op | source)
XLA Modules:
  0.0 71.5 jit_solution(8159843011540086850)
XLA Ops:
  0.6 0.0 copy-start.2
  0.6 0.0 copy-start
  0.7 2.1 %pack.1 = f32[32,24,128]{2,1,0:T(8,128)} custom-call(s32[16]{0:T(128)} %dest.1, s32[16,128]{1,0:T(8,128)} %bitcast.4, s32[16,128]{1,0:T(8,128)} %bitcast.6, f32[6,256]{1,0:T(8,128)} %motion.1, f32[3,2048]{1,0:T(4,128)} %offset.1, f32[8,2048]{1,0:T(8,128)} %refs_5_.1), custom_call_target="tpu_custom_call" | custom-call | tf_op jit(solution)/shard_map/pack/pallas_call | solution.py:548
  2.8 8.9 %all-to-all-start = ((f32[32,24,128]{2,1,0:T(8,128)}), f32[32,24,128]{2,1,0:T(8,128)S(1)}, u32[]{:S(2)}, u32[]{:S(2)}) async-start(f32[32,24,128]{2,1,0:T(8,128)} %pack.1), calls=%async_computation | async-start | bytes 786432 | tf_op jit(solution)/shard_map/all_to_all | solution.py:578
  11.8 0.6 moments.1
  12.4 0.1 pad_add_fusion.place.refs_0_
  12.4 13.2 %all-to-all-done.refs_0_.slots = f32[32,24,128]{2,1,0:T(8,128)S(1)} async-done(((f32[32,24,128]{2,1,0:T(8,128)}), f32[32,24,128]{2,1,0:T(8,128)S(1)}, u32[]{:S(2)}, u32[]{:S(2)}) %all-to-all-start) | async-done | bytes 393248 | tf_op jit(solution)/shard_map/all_to_all | solution.py:578
  25.6 5.3 %sample.1.pushed = f32[32,8,128]{2,1,0:T(8,128)} custom-call(f32[32,24,128]{2,1,0:T(8,128)S(1)} %all-to-all-done.refs_0_.slots, bf16[768,256]{1,0:T(8,128)(2,1)S(1)} %get-tuple-element.13.refs_1_), custom_call_target="tpu_custom_call" | custom-call | tf_op jit(solution)/shard_map/sample/pallas_call | solution.py:590
  31.0 4.0 %all-to-all-start.1 = ((f32[32,8,128]{2,1,0:T(8,128)}), f32[32,8,128]{2,1,0:T(8,128)S(1)}, u32[]{:S(2)}, u32[]{:S(2)}) async-start(f32[32,8,128]{2,1,0:T(8,128)} %sample.1.pushed), calls=%async_computation.1 | async-start | bytes 262144 | tf_op jit(solution)/shard_map/all_to_all | solution.py:598
  35.0 0.0 copy-start.1
  35.0 0.0 copy-start.3
  35.0 0.0 copy-start.7
  35.1 6.9 %spread.1 = (f32[19,4,32,128]{3,2,1,0:T(8,128)S(1)}, f32[5,32,128]{2,1,0:T(8,128)S(1)}, f32[5,32,128]{2,1,0:T(8,128)S(1)}, f32[24,128]{1,0:T(8,128)S(1)}, f32[24,128]{1,0:T(8,128)S(1)}) custom-call(s32[2]{0:T(128)S(1)} %pad_add_fusion.place.refs_0_, f32[32,24,128]{2,1,0:T(8,128)S(1)} %all-to-all-done.refs_0_.slots, f32[32,8,128]{2,1,0:T(8,128)} %sample.1.pushed, ...), custom_call_target="tpu_custom_call" | custom-call | flops 6000000000 | bytes 8000000 | tf_op jit(solution)/shard_map/spread/pallas_call | solution.py:600
  41.9 0.3 collective-permute-start
  42.2 5.5 %collective-permute-start.1 = (f32[5,32,128]{2,1,0:T(8,128)S(1)}, f32[5,32,128]{2,1,0:T(8,128)S(1)}, u32[]{:S(2)}, u32[]{:S(2)}) collective-permute-start(f32[5,32,128]{2,1,0:T(8,128)S(1)} %get-tuple-element.16), channel_id=1, source_target_pairs={{0,248},{8,16},{16,8},{24,32},{32,24},{40,48},{48,40},{56,64},{64,... | collective-permute-start | bytes 245768 | tf_op jit(solution)/shard_map/ppermute | solution.py:629
  47.7 0.0 all-to-all-done.1.returned
  47.8 1.0 %grain.1.refs_5_.partial = f32[8,256]{1,0:T(8,128)S(1)} custom-call(s32[16]{0:T(128)S(1)} %copy-done.7, s32[16,128]{1,0:T(8,128)S(1)} %bitcast.5, f32[3,2048]{1,0:T(4,128)S(1)} %copy-done.1, f32[32,8,128]{2,1,0:T(8,128)S(1)} %all-to-all-done.1.returned, f32[24,128]{1,0:T(8,128)S(1)} %get-tuple-element.18.after.refs_3_), custom_call_target="tpu_custom_call" | custom-call | tf_op jit(solution)/shard_map/grain/pallas_call | solution.py:619
  48.8 0.0 collective-permute-done.near_x.refs_1_
  48.8 1.3 %collective-permute-done.1.far_x.refs_2_ = f32[5,32,128]{2,1,0:T(8,128)S(1)} collective-permute-done((f32[5,32,128]{2,1,0:T(8,128)S(1)}, f32[5,32,128]{2,1,0:T(8,128)S(1)}, u32[]{:S(2)}, u32[]{:S(2)}) %collective-permute-start.1) | collective-permute-done | bytes 81952 | tf_op jit(solution)/shard_map/ppermute | solution.py:629
  50.2 0.5 edge.1
  50.7 1.3 %collective-permute-start.2 = (f32[40,128]{1,0:T(8,128)S(1)}, f32[40,128]{1,0:T(8,128)S(1)}, u32[]{:S(2)}, u32[]{:S(2)}) collective-permute-start(f32[40,128]{1,0:T(8,128)S(1)} %get-tuple-element.20), channel_id=1, source_target_pairs={{0,1},{1,0},{2,3},{3,2},{4,5},{5,4},{6,7},{7,6},{8,9},{9,8},{10,11... | collective-permute-start | bytes 61448 | tf_op jit(solution)/shard_map/ppermute | solution.py:641
  52.0 0.0 collective-permute-start.3
  52.0 2.6 %collective-permute-done.2.near_y = f32[40,128]{1,0:T(8,128)S(1)} collective-permute-done((f32[40,128]{1,0:T(8,128)S(1)}, f32[40,128]{1,0:T(8,128)S(1)}, u32[]{:S(2)}, u32[]{:S(2)}) %collective-permute-start.2) | collective-permute-done | bytes 20512 | tf_op jit(solution)/shard_map/ppermute | solution.py:641
  54.6 5.1 %collective-permute-start.6 = (f32[8,256]{1,0:T(8,128)S(1)}, f32[8,256]{1,0:T(8,128)S(1)}, u32[]{:S(2)}, u32[]{:S(2)}) collective-permute-start(f32[8,256]{1,0:T(8,128)S(1)} %pair.1.refs_1_), channel_id=1, source_target_pairs={{0,6},{1,7},{2,4},{3,5},{4,2},{5,3},{6,0},{7,1},{8,14},{9,15},{10,... | collective-permute-start | bytes 24584 | tf_op jit(solution)/shard_map/ppermute | solution.py:652
  59.7 4.5 %collective-permute-start.5 = (f32[8,256]{1,0:T(8,128)S(1)}, f32[8,256]{1,0:T(8,128)S(1)}, u32[]{:S(2)}, u32[]{:S(2)}) collective-permute-start(f32[8,256]{1,0:T(8,128)S(1)} %pair.1.refs_1_), channel_id=1, source_target_pairs={{0,4},{1,5},{2,6},{3,7},{4,0},{5,1},{6,2},{7,3},{8,12},{9,13},{10,... | collective-permute-start | bytes 24584 | tf_op jit(solution)/shard_map/ppermute | solution.py:652
  64.2 0.0 collective-permute-start.4
  64.2 1.7 %stream.1 = (f32[19,4,32,128]{3,2,1,0:T(8,128)}, f32[10,4,8,128]{3,2,1,0:T(8,128)S(1)}) custom-call(s32[2]{0:T(128)S(1)} %pad_add_fusion.place.refs_0_, f32[19,4,32,128]{3,2,1,0:T(8,128)S(1)} %get-tuple-element.14.collided, f32[5,32,128]{2,1,0:T(8,128)S(1)} %collective-permute-done.near_x.refs_1_, f32[5,32,128]{2,1,0:T(8,128)S(1)} %collective-permute-done.1.far_x.refs_2_), custom_call_target="tpu_custom_call" | custom-call | flops 20000000 | bytes 4000000 | tf_op jit(solution)/shard_map/stream/pallas_call | solution.py:654
  66.0 0.0 collective-permute-done.3.far_y
  66.0 0.0 collective-permute-done.6.refs_4_
  66.0 1.3 %collective-permute-done.5.refs_3_ = f32[8,256]{1,0:T(8,128)S(1)} collective-permute-done((f32[8,256]{1,0:T(8,128)S(1)}, f32[8,256]{1,0:T(8,128)S(1)}, u32[]{:S(2)}, u32[]{:S(2)}) %collective-permute-start.5) | collective-permute-done | bytes 8224 | tf_op jit(solution)/shard_map/ppermute | solution.py:652
  67.3 2.1 %collective-permute-done.4.refs_2_ = f32[8,256]{1,0:T(8,128)S(1)} collective-permute-done((f32[8,256]{1,0:T(8,128)S(1)}, f32[8,256]{1,0:T(8,128)S(1)}, u32[]{:S(2)}, u32[]{:S(2)}) %collective-permute-start.4) | collective-permute-done | bytes 8224 | tf_op jit(solution)/shard_map/ppermute | solution.py:652
  69.4 1.9 %rim.1 = (f32[19,4,32,128]{3,2,1,0:T(8,128)}, f32[6,256]{1,0:T(8,128)}) custom-call(s32[2]{0:T(128)S(1)} %pad_add_fusion.place.refs_0_, f32[10,4,8,128]{3,2,1,0:T(8,128)S(1)} %get-tuple-element.17.strips, f32[40,128]{1,0:T(8,128)S(1)} %collective-permute-done.2.near_y, f32[24,128]{1,0:T(8,128)S(1)} %collective-permute-done.3.far_y, ...), custom_call_target="tpu_custom_call", output_to_operand_aliasing={{0}: (9, {})} | custom-call | tf_op jit(solution)/shard_map/rim/pallas_call | solution.py:671
  (12 shorter events, 0.0 us)
Async XLA Ops:
  0.6 11.1 %copy-start.2 = (f32[6,256]{1,0:T(8,128)S(1)}, f32[6,256]{1,0:T(8,128)}, u32[]{:S(2)}) copy-start(f32[6,256]{1,0:T(8,128)} %motion.1) | copy-start | bytes 18436
  0.6 11.1 %copy-start = (f32[19,4,32,128]{3,2,1,0:T(8,128)S(1)}, f32[19,4,32,128]{3,2,1,0:T(8,128)}, u32[]{:S(2)}) copy-start(f32[19,4,32,128]{3,2,1,0:T(8,128)} %populations.3) | copy-start | bytes 3735556
  0.7 11.1 %copy-start.4 = (f32[3,512]{1,0:T(4,128)S(1)}, f32[3,512]{1,0:T(4,128)}, u32[]{:S(2)}) copy-start(f32[3,512]{1,0:T(4,128)} %rest.1) | copy-start | bytes 18436
  0.7 11.1 %copy-start.5 = (s32[2,512]{1,0:T(2,128)S(1)}, s32[2,512]{1,0:T(2,128)}, u32[]{:S(2)}) copy-start(s32[2,512]{1,0:T(2,128)} %pairs.1) | copy-start | bytes 12292
  0.7 11.1 %copy-start.6 = (f32[3,256]{1,0:T(4,128)S(1)}, f32[3,256]{1,0:T(4,128)}, u32[]{:S(2)}) copy-start(f32[3,256]{1,0:T(4,128)} %position.1) | copy-start | bytes 9220
  2.8 22.9 %all-to-all-start = ((f32[32,24,128]{2,1,0:T(8,128)}), f32[32,24,128]{2,1,0:T(8,128)S(1)}, u32[]{:S(2)}, u32[]{:S(2)}) async-start(f32[32,24,128]{2,1,0:T(8,128)} %pack.1), calls=%async_computation | async-start | bytes 786432 | tf_op jit(solution)/shard_map/all_to_all | solution.py:578
  31.0 16.8 %all-to-all-start.1 = ((f32[32,8,128]{2,1,0:T(8,128)}), f32[32,8,128]{2,1,0:T(8,128)S(1)}, u32[]{:S(2)}, u32[]{:S(2)}) async-start(f32[32,8,128]{2,1,0:T(8,128)} %sample.1.pushed), calls=%async_computation.1 | async-start | bytes 262144 | tf_op jit(solution)/shard_map/all_to_all | solution.py:598
  35.0 12.7 %copy-start.1 = (f32[3,2048]{1,0:T(4,128)S(1)}, f32[3,2048]{1,0:T(4,128)}, u32[]{:S(2)}) copy-start(f32[3,2048]{1,0:T(4,128)} %offset.1) | copy-start | bytes 73732
  35.0 12.7 %copy-start.3 = (s32[2048]{0:T(1024)S(1)}, s32[2048]{0:T(1024)}, u32[]{:S(2)}) copy-start(s32[2048]{0:T(1024)} %param.13) | copy-start | bytes 24580
  35.0 12.7 %copy-start.7 = (s32[16]{0:T(128)S(1)}, s32[16]{0:T(128)}, u32[]{:S(2)}) copy-start(s32[16]{0:T(128)} %dest.1) | copy-start | bytes 196
  41.9 6.9 %collective-permute-start = (f32[5,32,128]{2,1,0:T(8,128)S(1)}, f32[5,32,128]{2,1,0:T(8,128)S(1)}, u32[]{:S(2)}, u32[]{:S(2)}) collective-permute-start(f32[5,32,128]{2,1,0:T(8,128)S(1)} %get-tuple-element.15), channel_id=1, source_target_pairs={{0,8},{8,0},{16,24},{24,16},{32,40},{40,32},{48,56},{56,48},{64,72... | collective-permute-start | bytes 245768 | tf_op jit(solution)/shard_map/ppermute | solution.py:628
  42.2 8.0 %collective-permute-start.1 = (f32[5,32,128]{2,1,0:T(8,128)S(1)}, f32[5,32,128]{2,1,0:T(8,128)S(1)}, u32[]{:S(2)}, u32[]{:S(2)}) collective-permute-start(f32[5,32,128]{2,1,0:T(8,128)S(1)} %get-tuple-element.16), channel_id=1, source_target_pairs={{0,248},{8,16},{16,8},{24,32},{32,24},{40,48},{48,40},{56,64},{64,... | collective-permute-start | bytes 245768 | tf_op jit(solution)/shard_map/ppermute | solution.py:629
  50.7 3.9 %collective-permute-start.2 = (f32[40,128]{1,0:T(8,128)S(1)}, f32[40,128]{1,0:T(8,128)S(1)}, u32[]{:S(2)}, u32[]{:S(2)}) collective-permute-start(f32[40,128]{1,0:T(8,128)S(1)} %get-tuple-element.20), channel_id=1, source_target_pairs={{0,1},{1,0},{2,3},{3,2},{4,5},{5,4},{6,7},{7,6},{8,9},{9,8},{10,11... | collective-permute-start | bytes 61448 | tf_op jit(solution)/shard_map/ppermute | solution.py:641
  52.0 13.9 %collective-permute-start.3 = (f32[24,128]{1,0:T(8,128)S(1)}, f32[24,128]{1,0:T(8,128)S(1)}, u32[]{:S(2)}, u32[]{:S(2)}) collective-permute-start(f32[24,128]{1,0:T(8,128)S(1)} %get-tuple-element.21), channel_id=1, source_target_pairs={{0,7},{1,2},{2,1},{3,4},{4,3},{5,6},{6,5},{7,0},{8,15},{9,10},{10,... | collective-permute-start | bytes 36872 | tf_op jit(solution)/shard_map/ppermute | solution.py:642
  54.6 11.4 %collective-permute-start.6 = (f32[8,256]{1,0:T(8,128)S(1)}, f32[8,256]{1,0:T(8,128)S(1)}, u32[]{:S(2)}, u32[]{:S(2)}) collective-permute-start(f32[8,256]{1,0:T(8,128)S(1)} %pair.1.refs_1_), channel_id=1, source_target_pairs={{0,6},{1,7},{2,4},{3,5},{4,2},{5,3},{6,0},{7,1},{8,14},{9,15},{10,... | collective-permute-start | bytes 24584 | tf_op jit(solution)/shard_map/ppermute | solution.py:652
  59.7 7.6 %collective-permute-start.5 = (f32[8,256]{1,0:T(8,128)S(1)}, f32[8,256]{1,0:T(8,128)S(1)}, u32[]{:S(2)}, u32[]{:S(2)}) collective-permute-start(f32[8,256]{1,0:T(8,128)S(1)} %pair.1.refs_1_), channel_id=1, source_target_pairs={{0,4},{1,5},{2,6},{3,7},{4,0},{5,1},{6,2},{7,3},{8,12},{9,13},{10,... | collective-permute-start | bytes 24584 | tf_op jit(solution)/shard_map/ppermute | solution.py:652
  64.2 5.2 %collective-permute-start.4 = (f32[8,256]{1,0:T(8,128)S(1)}, f32[8,256]{1,0:T(8,128)S(1)}, u32[]{:S(2)}, u32[]{:S(2)}) collective-permute-start(f32[8,256]{1,0:T(8,128)S(1)} %pair.1.refs_1_), channel_id=1, source_target_pairs={{0,2},{1,3},{2,0},{3,1},{4,6},{5,7},{6,4},{7,5},{8,10},{9,11},{10,... | collective-permute-start | bytes 24584 | tf_op jit(solution)/shard_map/ppermute | solution.py:652

commit v3 on v2

--- a/solution.py
+++ b/solution.py
@@ -79,6 +79,10 @@
     return high, low
 
 
+def is_even(place, axis, rows):
+    return jnp.broadcast_to(place[8 * axis : 8 * axis + 1, :], (rows, place.shape[1])) == 0
+
+
 def thirds(value):
     high = value.astype(BF16)
     rest = value - high.astype(F32)
@@ -329,33 +333,42 @@
             for axis in range(3):
                 first = axis * size_z + x * size_y + y
                 forcing.append(total[first : first + CHUNK, :size_z])
-            velocity = [(momentum[a] + 0.5 * forcing[a]) * inverse for a in range(3)]
+            flux = [momentum[a] + 0.5 * forcing[a] for a in range(3)]
+            velocity = [flux[a] * inverse for a in range(3)]
             speed_square = sum_of([v * v for v in velocity])
             flow_force = sum_of([velocity[a] * forcing[a] for a in range(3)])
-            rest_flow = 1.0 - 1.5 * speed_square
-            rest_force = -3.0 * flow_force
+            flow_part = lattice_weight((1, 1, 0)) / RELAX_TIME
+            force_part = factor * lattice_weight((1, 1, 0))
+            base = (flow_part * density) * (1.0 - 1.5 * speed_square) - (
+                3.0 * force_part
+            ) * flow_force
+            pushes = [(3.0 * force_part) * forcing[a] for a in range(3)]
+            odd_field = [(3.0 * flow_part) * flux[a] + pushes[a] for a in range(3)]
+            even_field = [odd_field[a] + pushes[a] for a in range(3)]
+            speed = [1.5 * velocity[a] for a in range(3)]
+            keep = 1.0 - 1.0 / RELAX_TIME
             for number, vector in enumerate(LATTICE):
-                weight = lattice_weight(vector)
-                flow = rest_flow
-                push = rest_force
-                if any(vector):
-                    along_flow = project(vector, velocity)
-                    along_force = project(vector, forcing)
-                    flow = flow + along_flow * (3.0 + 4.5 * along_flow)
-                    push = push + along_force * (3.0 + 9.0 * along_flow)
-                collided[number, x, rows] = (
-                    (1.0 - 1.0 / RELAX_TIME) * current[number]
-                    + (weight / RELAX_TIME) * density * flow
-                    + (factor * weight) * push
-                )
-
-    even_x = place[0] == 0
+                if OPPOSITE[number] < number:
+                    continue
+                if number == 0:
+                    collided[0, x, rows] = keep * current[0] + 12.0 * base
+                    continue
+                odd = project(vector, odd_field)
+                even = base + project(vector, speed) * project(vector, even_field)
+                if number < 7:
+                    odd = odd + odd
+                    even = even + even
+                other = OPPOSITE[number]
+                collided[number, x, rows] = keep * current[number] + (even + odd)
+                collided[other, x, rows] = keep * current[other] + (even - odd)
+
+    even_x = is_even(place, 0, size_y)
     for index, (up, down) in enumerate(zip(UP_X, DOWN_X)):
         top = collided[up, size_x - 1]
         bottom = collided[down, 0]
         near_x[index] = jnp.where(even_x, top, bottom)
         far_x[index] = jnp.where(even_x, bottom, top)
-    even_y = place[1] == 0
+    even_y = is_even(place, 1, 1)
     for index, (up, down) in enumerate(zip(UP_Y, DOWN_Y)):
         for x in range(size_x):
             top = collided[up, x, size_y - 1 : size_y]
@@ -369,11 +382,11 @@
 
 
 def edge_kernel(
-    place, near_x, far_x, near_y, far_y, partial, near_out, far_out, *, size_x
+    place, near_x, far_x, near_y, far_y, partial, across, near_out, far_out, total, *, size_x
 ):
     size_y = near_x.shape[1]
     filled = len(UP_Y) * size_x
-    even_x = place[0] == 0
+    even_x = is_even(place, 0, 1)
     from_x = lambda number, y: jnp.where(
         even_x, far_x[UP_X.index(number), y : y + 1], near_x[UP_X.index(number), y : y + 1]
     )
@@ -383,13 +396,16 @@
     top = size_y - 1
     up = jnp.concatenate([from_x(LATTICE.index((1, 1, 0)), top), to_x(LATTICE.index((-1, 1, 0)), top)], axis=0)
     down = jnp.concatenate([from_x(LATTICE.index((1, -1, 0)), 0), to_x(LATTICE.index((-1, -1, 0)), 0)], axis=0)
-    even_y = place[1] == 0
+    even_y = is_even(place, 1, 2)
     near_out[:EDGE_ROWS] = near_y[...]
     far_out[...] = far_y[...]
     width = near_out.shape[1]
     for part in range(partial.shape[1] // width):
         first = EDGE_ROWS + 8 * part
-        near_out[first : first + 8] = partial[:, part * width : (part + 1) * width]
+        span = slice(part * width, (part + 1) * width)
+        value = partial[:, span] + across[:, span]
+        total[:, span] = value
+        near_out[first : first + 8] = value
     near_out[filled : filled + 2] = jnp.where(even_y, up, down)
     far_out[filled : filled + 2] = jnp.where(even_y, down, up)
 
@@ -416,15 +432,22 @@
     return value
 
 
-def stream_kernel(place, collided, near_x, far_x, out, strips, stage, sems):
+def stream_kernel(place, collided, near_x, far_x, near_y, far_y, out, stage, sems):
     quantity, size_x, size_y, size_z = collided.shape
+    row = lax.broadcasted_iota(jnp.int32, (size_y, size_z), 0)
     lane = lax.broadcasted_iota(jnp.int32, (size_y, size_z), 1)
-    even_x = place[0] == 0
+    even_x = is_even(place, 0, size_y)
+    even_y = is_even(place, 1, EDGE_ROWS)
+    filled = len(UP_Y) * size_x
+    near, far = near_y[:EDGE_ROWS], far_y[...]
+    from_y = jnp.where(even_y, far, near)
+    to_y = jnp.where(even_y, near, far)
     copies = []
-    for x in (1, 2, 0, 3):
+    for x in range(size_x):
         for number, vector in enumerate(LATTICE):
             source = x - vector[0]
-            if 0 <= source < size_x:
+            inside = 0 <= source < size_x
+            if inside:
                 value = collided[number, source]
             elif vector[0] == 1:
                 index = UP_X.index(number)
@@ -433,7 +456,17 @@
                 index = DOWN_X.index(number)
                 value = jnp.where(even_x, near_x[index], far_x[index])
             if vector[1]:
-                value = pltpu.roll(value, 1 if vector[1] == 1 else size_y - 1, 0)
+                face = from_y if vector[1] == 1 else to_y
+                column = UP_Y if vector[1] == 1 else DOWN_Y
+                if inside:
+                    line = column.index(number) * size_x + source
+                else:
+                    line = filled if vector[0] == 1 else filled + 1
+                ghost = face[line : line + 1]
+                if vector[1] == 1:
+                    value = jnp.where(row == 0, ghost, pltpu.roll(value, 1, 0))
+                else:
+                    value = jnp.where(row == size_y - 1, ghost, pltpu.roll(value, size_y - 1, 0))
             if vector[2]:
                 back = collided[OPPOSITE[number], x]
                 if vector[2] == 1:
@@ -441,10 +474,6 @@
                 else:
                     value = jnp.where(lane == size_z - 1, back, pltpu.roll(value, size_z - 1, 1))
             stage[number, x] = value
-            if vector[1] == 1:
-                strips[UP_Y.index(number), x] = value[:8]
-            elif vector[1] == -1:
-                strips[len(UP_Y) + DOWN_Y.index(number), x] = value[size_y - 8 :]
         copy = pltpu.make_async_copy(stage.at[:, x], out.at[:, x], sems.at[x])
         copy.start()
         copies.append(copy)
@@ -452,44 +481,9 @@
         copy.wait()
 
 
-def rim_kernel(place, strips, near_y, far_y, *refs):
-    parts, (given, out, load, stage, sems) = refs[:-5], refs[-5:]
-    size_x, size_y, size_z = out.shape[1:]
-    row = lax.broadcasted_iota(jnp.int32, (8, size_z), 0)
-    lane = lax.broadcasted_iota(jnp.int32, (8, size_z), 1)
-    even_y = place[1] == 0
-    filled = len(UP_Y) * size_x
-    near, far = near_y[:EDGE_ROWS], far_y[...]
-    from_y = jnp.where(even_y, far, near)
-    to_y = jnp.where(even_y, near, far)
-    copies = []
-    for group, (face, column, edge) in enumerate(((from_y, UP_Y, 0), (to_y, DOWN_Y, 7))):
-        for index, number in enumerate(column):
-            vector = LATTICE[number]
-            slot = group * len(UP_Y) + index
-            for x in range(size_x):
-                source = x - vector[0]
-                if 0 <= source < size_x:
-                    line = index * size_x + source
-                else:
-                    line = filled if vector[0] == 1 else filled + 1
-                ghost = jnp.broadcast_to(face[line : line + 1], (8, size_z))
-                replace = row == edge
-                if vector[2] == 1:
-                    ghost = pltpu.roll(ghost, 1, 1)
-                    replace = jnp.logical_and(replace, lane != 0)
-                elif vector[2] == -1:
-                    ghost = pltpu.roll(ghost, size_z - 1, 1)
-                    replace = jnp.logical_and(replace, lane != size_z - 1)
-                stage[slot, x] = jnp.where(replace, ghost, strips[slot, x])
-            rows = pl.ds(0 if edge == 0 else size_y - 8, 8)
-            copy = pltpu.make_async_copy(stage.at[slot], out.at[number, :, rows], sems.at[slot])
-            copy.start()
-            copies.append(copy)
-    total = sum_of([part[...] for part in parts])
+def load_kernel(bonded, first, second, load):
+    total = first[...] + second[...] + bonded[...]
     load[...] = total[: load.shape[0]]
-    for copy in copies:
-        copy.wait()
 
 
 def grain_kernel(dest, grain, offset, returned, after, partial, used):
@@ -544,7 +538,9 @@
     grain_blocks = marker_grain.reshape(blocks, MARKS)
     cell_blocks = marker_cell.reshape(blocks, MARKS)
 
-    place = jnp.stack([lax.axis_index("gx") & 1, lax.axis_index("gy") & 1]).astype(jnp.int32)
+    place = jnp.concatenate(
+        [jnp.full((8, size_z), lax.axis_index(axis) & 1, jnp.int32) for axis in ("gx", "gy")]
+    )
     outgoing = pl.pallas_call(
         pack_kernel,
         out_shape=shape((bricks, SLOT_ROWS, MARKS), F32),
@@ -606,7 +602,7 @@
             shape((EDGE_ROWS, size_z), F32),
             shape((EDGE_ROWS, size_z), F32),
         ],
-        in_specs=[SMEM] + [VMEM] * 3,
+        in_specs=[VMEM] * 4,
         out_specs=[VMEM] * 5,
         scratch_shapes=[pltpu.VMEM((3 * size_z, 2 * planes), F32)],
         compiler_params=params,
@@ -627,17 +623,19 @@
     )(block_dest, grain_blocks, marker_offset, returned, faces[2])
     near_x = lax.ppermute(faces[0], "gx", swap("gx", 0))
     far_x = lax.ppermute(faces[1], "gx", swap("gx", 1))
-    near_y, far_y = pl.pallas_call(
+    across = lax.ppermute(partial, "gy", cross(4))
+    near_y, far_y, total = pl.pallas_call(
         lambda *refs: edge_kernel(*refs, size_x=size_x),
         out_shape=[
             shape((EDGE_ROWS + 8 * slab // size_z, size_z), F32),
             shape((EDGE_ROWS, size_z), F32),
+            shape((8, slab), F32),
         ],
-        in_specs=[SMEM] + [VMEM] * 5,
-        out_specs=[VMEM] * 2,
+        in_specs=[VMEM] * 7,
+        out_specs=[VMEM] * 3,
         compiler_params=params,
         name="edge",
-    )(place, near_x, far_x, faces[2], faces[3], partial)
+    )(place, near_x, far_x, faces[2], faces[3], partial, across)
     near_y = lax.ppermute(near_y, "gy", swap("gy", 0))
     far_y = lax.ppermute(far_y, "gy", swap("gy", 1))
     total = pl.pallas_call(
@@ -647,18 +645,13 @@
         out_specs=VMEM,
         compiler_params=params,
         name="pair",
-    )(partial, near_y)
-    parts = [bonded, total]
-    parts += [lax.ppermute(total, "gy", cross(step)) for step in range(2, lax.axis_size("gy"), 2)]
-
-    streamed, strips = pl.pallas_call(
+    )(total, near_y)
+
+    populations_next = pl.pallas_call(
         stream_kernel,
-        out_shape=[
-            shape(populations.shape, F32),
-            shape((len(UP_Y) + len(DOWN_Y), size_x, 8, size_z), F32),
-        ],
-        in_specs=[SMEM] + [VMEM] * 3,
-        out_specs=[HBM, VMEM],
+        out_shape=shape(populations.shape, F32),
+        in_specs=[VMEM] * 6,
+        out_specs=HBM,
         scratch_shapes=[
             pltpu.VMEM(populations.shape, F32),
             pltpu.SemaphoreType.DMA((size_x,)),
@@ -666,21 +659,16 @@
         compiler_params=params,
         cost_estimate=pl.CostEstimate(flops=20000000, bytes_accessed=4000000, transcendentals=0),
         name="stream",
-    )(place, collided, near_x, far_x)
-
-    populations_next, grain_load = pl.pallas_call(
-        rim_kernel,
-        out_shape=[shape(populations.shape, F32), shape((6, slab), F32)],
-        in_specs=[SMEM] + [VMEM] * (3 + len(parts)) + [HBM],
-        out_specs=[HBM, VMEM],
-        scratch_shapes=[
-            pltpu.VMEM(strips.shape, F32),
-            pltpu.SemaphoreType.DMA((strips.shape[0],)),
-        ],
-        input_output_aliases={4 + len(parts): 0},
-        compiler_params=params,
-        name="rim",
-    )(place, strips, near_y, far_y, *parts, streamed)
+    )(place, collided, near_x, far_x, near_y, far_y)
+
+    grain_load = pl.pallas_call(
+        load_kernel,
+        out_shape=shape((6, slab), F32),
+        in_specs=[VMEM] * 3,
+        out_specs=VMEM,
+        compiler_params=params,
+        name="load",
+    )(bonded, total, lax.ppermute(total, "gy", cross(2)))
     return populations_next, grain_load
 
 

time: 71.8 us -> 69 us (0.961)
  the two profiles are of different devices: /device:TPU:4 before, /device:TPU:0 now
where the time goes in v3:
time: 69 us; the launch traced here: 67.9 us
  starting transfers between devices  29.4 us (43%)
  waiting for transfers between devices  20.3 us (29%)
  Pallas kernels  17.3 us (25%)
  between operations  0.81 us (1%)
    all_to_all x1, waiting for transfers between devices, shards(): lax.all_to_all(outgoing, 'gx', split_axis=0, concat_axis=0, tiled=True)  13.3 us
    all_to_all x1, starting transfers between devices, shards(): lax.all_to_all(outgoing, 'gx', split_axis=0, concat_axis=0, tiled=True)  7.19 us
    pallas_call x1, Pallas kernels, shards(): pl.pallas_call(spread_kernel, out_shape=[shape(populations.shape, F32), s...  6.52 us
    ppermute x1, starting transfers between devices, shards(): far_y = lax.ppermute(far_y, 'gy', swap('gy', 1))  6.01 us
    ppermute x1, starting transfers between devices, shards(): far_x = lax.ppermute(faces[1], 'gx', swap('gx', 1))  5.69 us
    pallas_call x1, Pallas kernels, shards(): pl.pallas_call(lambda *refs: sample_kernel(*refs, size=(size_x, size_y, s...  5.33 us
    ppermute x1, starting transfers between devices, shards(): across = lax.ppermute(partial, 'gy', cross(4))  4.56 us
    all_to_all x1, starting transfers between devices, shards(): lax.all_to_all(pushed, 'gx', split_axis=0, concat_axis=0, tiled=True)  3.86 us
  transfers between devices with their start and end apart: 8, of which 4 were waited for; matrix products, arithmetic and copies ran while one was open for 0% of the time, Pallas kernels for 14%

profile of v3, /device:TPU:0, one launch (start us, length us, event | category | flops | bytes accessed | tf_op | source)
XLA Modules:
  0.0 67.9 jit_solution(2972125295986744044)
XLA Ops:
  0.6 0.0 copy-start.2
  0.7 2.1 %pack.1 = f32[32,24,128]{2,1,0:T(8,128)} custom-call(s32[16]{0:T(128)} %dest.1, s32[16,128]{1,0:T(8,128)} %bitcast.2, s32[16,128]{1,0:T(8,128)} %bitcast.4, f32[6,256]{1,0:T(8,128)} %motion.1, f32[3,2048]{1,0:T(4,128)} %offset.1, f32[8,2048]{1,0:T(8,128)} %refs_5_.1), custom_call_target="tpu_custom_call" | custom-call | tf_op jit(solution)/shard_map/pack/pallas_call | solution.py:544
  2.8 7.2 %all-to-all-start = ((f32[32,24,128]{2,1,0:T(8,128)}), f32[32,24,128]{2,1,0:T(8,128)S(1)}, u32[]{:S(2)}, u32[]{:S(2)}) async-start(f32[32,24,128]{2,1,0:T(8,128)} %pack.1), calls=%async_computation | async-start | bytes 786432 | tf_op jit(solution)/shard_map/all_to_all | solution.py:574
  10.0 0.0 copy-done.2
  10.0 0.0 copy-done
  10.0 0.0 copy-done.6
  10.0 0.0 copy-done.5
  10.1 0.0 copy-done.4
  10.1 0.6 moments.1
  10.6 13.3 %all-to-all-done.refs_0_.slots = f32[32,24,128]{2,1,0:T(8,128)S(1)} async-done(((f32[32,24,128]{2,1,0:T(8,128)}), f32[32,24,128]{2,1,0:T(8,128)S(1)}, u32[]{:S(2)}, u32[]{:S(2)}) %all-to-all-start) | async-done | bytes 393248 | tf_op jit(solution)/shard_map/all_to_all | solution.py:574
  23.9 5.3 %sample.1.pushed = f32[32,8,128]{2,1,0:T(8,128)} custom-call(f32[32,24,128]{2,1,0:T(8,128)S(1)} %all-to-all-done.refs_0_.slots, bf16[768,256]{1,0:T(8,128)(2,1)S(1)} %get-tuple-element.12.refs_1_), custom_call_target="tpu_custom_call" | custom-call | tf_op jit(solution)/shard_map/sample/pallas_call | solution.py:586
  29.2 3.9 %all-to-all-start.1 = ((f32[32,8,128]{2,1,0:T(8,128)}), f32[32,8,128]{2,1,0:T(8,128)S(1)}, u32[]{:S(2)}, u32[]{:S(2)}) async-start(f32[32,8,128]{2,1,0:T(8,128)} %sample.1.pushed), calls=%async_computation.1 | async-start | bytes 262144 | tf_op jit(solution)/shard_map/all_to_all | solution.py:594
  33.1 0.1 concatenate.6.place.refs_0_
  33.2 6.5 %spread.1 = (f32[19,4,32,128]{3,2,1,0:T(8,128)S(1)}, f32[5,32,128]{2,1,0:T(8,128)S(1)}, f32[5,32,128]{2,1,0:T(8,128)S(1)}, f32[24,128]{1,0:T(8,128)S(1)}, f32[24,128]{1,0:T(8,128)S(1)}) custom-call(s32[16,128]{1,0:T(8,128)S(1)} %concatenate.6.place.refs_0_, f32[32,24,128]{2,1,0:T(8,128)S(1)} %all-to-all-done.refs_0_.slots, f32[32,8,128]{2,1,0:T(8,128)} %sample.1.pushed, ...), custom_call_target="tpu_custom_call" | custom-call | flops 6000000000 | bytes 8000000 | tf_op jit(solution)/shard_map/spread/pallas_call | solution.py:596
  39.7 0.5 collective-permute-start
  40.2 5.7 %collective-permute-start.1 = (f32[5,32,128]{2,1,0:T(8,128)S(1)}, f32[5,32,128]{2,1,0:T(8,128)S(1)}, u32[]{:S(2)}, u32[]{:S(2)}) collective-permute-start(f32[5,32,128]{2,1,0:T(8,128)S(1)} %get-tuple-element.15), channel_id=1, source_target_pairs={{0,248},{8,16},{16,8},{24,32},{32,24},{40,48},{48,40},{56,64},{64,... | collective-permute-start | bytes 245768 | tf_op jit(solution)/shard_map/ppermute | solution.py:625
  45.9 0.0 all-to-all-done.1.returned
  45.9 0.0 copy-done.3
  45.9 0.0 copy-done.7
  45.9 1.0 %grain.1.refs_5_ = f32[8,256]{1,0:T(8,128)S(1)} custom-call(s32[16]{0:T(128)S(1)} %copy-done.7, s32[16,128]{1,0:T(8,128)S(1)} %bitcast.3, f32[3,2048]{1,0:T(4,128)S(1)} %copy-done.1, f32[32,8,128]{2,1,0:T(8,128)S(1)} %all-to-all-done.1.returned, f32[24,128]{1,0:T(8,128)S(1)} %get-tuple-element.16.after.refs_3_), custom_call_target="tpu_custom_call" | custom-call | tf_op jit(solution)/shard_map/grain/pallas_call | solution.py:615
  46.9 4.6 %collective-permute-start.2 = (f32[8,256]{1,0:T(8,128)S(1)}, f32[8,256]{1,0:T(8,128)S(1)}, u32[]{:S(2)}, u32[]{:S(2)}) collective-permute-start(f32[8,256]{1,0:T(8,128)S(1)} %grain.1.refs_5_), channel_id=1, source_target_pairs={{0,4},{1,5},{2,6},{3,7},{4,0},{5,1},{6,2},{7,3},{8,12},{9,13},{10,... | collective-permute-start | bytes 24584 | tf_op jit(solution)/shard_map/ppermute | solution.py:626
  51.5 0.0 collective-permute-done.refs_1_.near_x
  51.5 0.0 collective-permute-done.1.refs_2_.far_x
  51.5 3.1 %collective-permute-done.2.refs_6_ = f32[8,256]{1,0:T(8,128)S(1)} collective-permute-done((f32[8,256]{1,0:T(8,128)S(1)}, f32[8,256]{1,0:T(8,128)S(1)}, u32[]{:S(2)}, u32[]{:S(2)}) %collective-permute-start.2) | collective-permute-done | bytes 8224 | tf_op jit(solution)/shard_map/ppermute | solution.py:626
  54.6 1.6 %collective-permute-start.3 = (f32[40,128]{1,0:T(8,128)S(1)}, f32[40,128]{1,0:T(8,128)S(1)}, u32[]{:S(2)}, u32[]{:S(2)}) collective-permute-start(f32[40,128]{1,0:T(8,128)S(1)} %get-tuple-element.18), channel_id=1, source_target_pairs={{0,1},{1,0},{2,3},{3,2},{4,5},{5,4},{6,7},{7,6},{8,9},{9,8},{10,11... | collective-permute-start | bytes 61448 | tf_op jit(solution)/shard_map/ppermute | solution.py:639
  56.2 6.0 %collective-permute-start.4 = (f32[24,128]{1,0:T(8,128)S(1)}, f32[24,128]{1,0:T(8,128)S(1)}, u32[]{:S(2)}, u32[]{:S(2)}) collective-permute-start(f32[24,128]{1,0:T(8,128)S(1)} %get-tuple-element.19), channel_id=1, source_target_pairs={{0,7},{1,2},{2,1},{3,4},{4,3},{5,6},{6,5},{7,0},{8,15},{9,10},{10,... | collective-permute-start | bytes 36872 | tf_op jit(solution)/shard_map/ppermute | solution.py:640
  62.2 0.0 collective-permute-done.3.near_y
  62.2 0.0 collective-permute-start.5
  62.2 3.7 %collective-permute-done.4.far_y = f32[24,128]{1,0:T(8,128)S(1)} collective-permute-done((f32[24,128]{1,0:T(8,128)S(1)}, f32[24,128]{1,0:T(8,128)S(1)}, u32[]{:S(2)}, u32[]{:S(2)}) %collective-permute-start.4) | collective-permute-done | bytes 12320 | tf_op jit(solution)/shard_map/ppermute | solution.py:640
  65.9 1.2 %stream.1 = f32[19,4,32,128]{3,2,1,0:T(8,128)} custom-call(s32[16,128]{1,0:T(8,128)S(1)} %concatenate.6.place.refs_0_, f32[19,4,32,128]{3,2,1,0:T(8,128)S(1)} %get-tuple-element.13.collided, f32[5,32,128]{2,1,0:T(8,128)S(1)} %collective-permute-done.refs_1_.near_x, f32[5,32,128]{2,1,0:T(8,128)S(1)} %collective-permute-done.1.refs_2_.far_x, ...), custom_call_target="tpu_custom_call" | custom-call | flops 20000000 | bytes 4000000 | tf_op jit(solution)/shard_map/stream/pallas_call | solution.py:650
  67.0 0.3 collective-permute-done.5.second
  67.3 0.6 load.1
  (12 shorter events, 0.0 us)
Async XLA Ops:
  0.6 9.4 %copy-start.2 = (f32[6,256]{1,0:T(8,128)S(1)}, f32[6,256]{1,0:T(8,128)}, u32[]{:S(2)}) copy-start(f32[6,256]{1,0:T(8,128)} %motion.1) | copy-start | bytes 18436
  0.6 9.4 %copy-start = (f32[19,4,32,128]{3,2,1,0:T(8,128)S(1)}, f32[19,4,32,128]{3,2,1,0:T(8,128)}, u32[]{:S(2)}) copy-start(f32[19,4,32,128]{3,2,1,0:T(8,128)} %populations.3) | copy-start | bytes 3735556
  0.7 9.4 %copy-start.6 = (f32[3,256]{1,0:T(4,128)S(1)}, f32[3,256]{1,0:T(4,128)}, u32[]{:S(2)}) copy-start(f32[3,256]{1,0:T(4,128)} %position.1) | copy-start | bytes 9220
  0.7 9.4 %copy-start.5 = (s32[2,512]{1,0:T(2,128)S(1)}, s32[2,512]{1,0:T(2,128)}, u32[]{:S(2)}) copy-start(s32[2,512]{1,0:T(2,128)} %pairs.1) | copy-start | bytes 12292
  0.7 9.4 %copy-start.4 = (f32[3,512]{1,0:T(4,128)S(1)}, f32[3,512]{1,0:T(4,128)}, u32[]{:S(2)}) copy-start(f32[3,512]{1,0:T(4,128)} %rest.1) | copy-start | bytes 18436
  2.8 21.1 %all-to-all-start = ((f32[32,24,128]{2,1,0:T(8,128)}), f32[32,24,128]{2,1,0:T(8,128)S(1)}, u32[]{:S(2)}, u32[]{:S(2)}) async-start(f32[32,24,128]{2,1,0:T(8,128)} %pack.1), calls=%async_computation | async-start | bytes 786432 | tf_op jit(solution)/shard_map/all_to_all | solution.py:574
  29.2 16.6 %all-to-all-start.1 = ((f32[32,8,128]{2,1,0:T(8,128)}), f32[32,8,128]{2,1,0:T(8,128)S(1)}, u32[]{:S(2)}, u32[]{:S(2)}) async-start(f32[32,8,128]{2,1,0:T(8,128)} %sample.1.pushed), calls=%async_computation.1 | async-start | bytes 262144 | tf_op jit(solution)/shard_map/all_to_all | solution.py:594
  33.2 12.7 %copy-start.1 = (f32[3,2048]{1,0:T(4,128)S(1)}, f32[3,2048]{1,0:T(4,128)}, u32[]{:S(2)}) copy-start(f32[3,2048]{1,0:T(4,128)} %offset.1) | copy-start | bytes 73732
  33.2 12.7 %copy-start.3 = (s32[2048]{0:T(1024)S(1)}, s32[2048]{0:T(1024)}, u32[]{:S(2)}) copy-start(s32[2048]{0:T(1024)} %param.13) | copy-start | bytes 24580
  33.2 12.7 %copy-start.7 = (s32[16]{0:T(128)S(1)}, s32[16]{0:T(128)}, u32[]{:S(2)}) copy-start(s32[16]{0:T(128)} %dest.1) | copy-start | bytes 196
  39.7 11.8 %collective-permute-start = (f32[5,32,128]{2,1,0:T(8,128)S(1)}, f32[5,32,128]{2,1,0:T(8,128)S(1)}, u32[]{:S(2)}, u32[]{:S(2)}) collective-permute-start(f32[5,32,128]{2,1,0:T(8,128)S(1)} %get-tuple-element.14), channel_id=1, source_target_pairs={{0,8},{8,0},{16,24},{24,16},{32,40},{40,32},{48,56},{56,48},{64,72... | collective-permute-start | bytes 245768 | tf_op jit(solution)/shard_map/ppermute | solution.py:624
  40.2 11.3 %collective-permute-start.1 = (f32[5,32,128]{2,1,0:T(8,128)S(1)}, f32[5,32,128]{2,1,0:T(8,128)S(1)}, u32[]{:S(2)}, u32[]{:S(2)}) collective-permute-start(f32[5,32,128]{2,1,0:T(8,128)S(1)} %get-tuple-element.15), channel_id=1, source_target_pairs={{0,248},{8,16},{16,8},{24,32},{32,24},{40,48},{48,40},{56,64},{64,... | collective-permute-start | bytes 245768 | tf_op jit(solution)/shard_map/ppermute | solution.py:625
  46.9 7.6 %collective-permute-start.2 = (f32[8,256]{1,0:T(8,128)S(1)}, f32[8,256]{1,0:T(8,128)S(1)}, u32[]{:S(2)}, u32[]{:S(2)}) collective-permute-start(f32[8,256]{1,0:T(8,128)S(1)} %grain.1.refs_5_), channel_id=1, source_target_pairs={{0,4},{1,5},{2,6},{3,7},{4,0},{5,1},{6,2},{7,3},{8,12},{9,13},{10,... | collective-permute-start | bytes 24584 | tf_op jit(solution)/shard_map/ppermute | solution.py:626
  54.6 7.6 %collective-permute-start.3 = (f32[40,128]{1,0:T(8,128)S(1)}, f32[40,128]{1,0:T(8,128)S(1)}, u32[]{:S(2)}, u32[]{:S(2)}) collective-permute-start(f32[40,128]{1,0:T(8,128)S(1)} %get-tuple-element.18), channel_id=1, source_target_pairs={{0,1},{1,0},{2,3},{3,2},{4,5},{5,4},{6,7},{7,6},{8,9},{9,8},{10,11... | collective-permute-start | bytes 61448 | tf_op jit(solution)/shard_map/ppermute | solution.py:639
  56.2 9.7 %collective-permute-start.4 = (f32[24,128]{1,0:T(8,128)S(1)}, f32[24,128]{1,0:T(8,128)S(1)}, u32[]{:S(2)}, u32[]{:S(2)}) collective-permute-start(f32[24,128]{1,0:T(8,128)S(1)} %get-tuple-element.19), channel_id=1, source_target_pairs={{0,7},{1,2},{2,1},{3,4},{4,3},{5,6},{6,5},{7,0},{8,15},{9,10},{10,... | collective-permute-start | bytes 36872 | tf_op jit(solution)/shard_map/ppermute | solution.py:640
  62.2 5.2 %collective-permute-start.5 = (f32[8,256]{1,0:T(8,128)S(1)}, f32[8,256]{1,0:T(8,128)S(1)}, u32[]{:S(2)}, u32[]{:S(2)}) collective-permute-start(f32[8,256]{1,0:T(8,128)S(1)} %pair.1.first), channel_id=1, source_target_pairs={{0,2},{1,3},{2,0},{3,1},{4,6},{5,7},{6,4},{7,5},{8,10},{9,11},{10,... | collective-permute-start | bytes 24584 | tf_op jit(solution)/shard_map/ppermute | solution.py:671

commit v4 on v3

--- a/solution.py
+++ b/solution.py
@@ -13,7 +13,8 @@
 SAMPLE_GROUP = 2
 SAMPLE_UNROLL = 16
 SPREAD_GROUP = 8
-SPREAD_UNROLL = 4
+SPREAD_FEW = 12
+SPREAD_FEW_GROUP = 6
 CHUNK = 8
 
 
@@ -208,9 +209,12 @@
     bond_part(pairs, rest, position, motion, bonded)
 
 
-def marker_places(slots, size_x, size_y, size_z):
+def source_markers(slots):
     cells = jnp.concatenate([slots[19:20], slots[23:24]], axis=1).astype(jnp.int32)
-    weight = jnp.concatenate([slots[0:8], slots[8:16]], axis=1)
+    return cells, jnp.concatenate([slots[0:8], slots[8:16]], axis=1)
+
+
+def marker_places(cells, weight, size_x, size_y, size_z):
     place_x = lax.shift_right_logical(cells, (size_y * size_z).bit_length() - 1)
     place_y = lax.shift_right_logical(cells, size_z.bit_length() - 1) & (size_y - 1)
     place_z = cells & (size_z - 1)
@@ -247,7 +251,7 @@
     return [jnp.concatenate(table, axis=0) for table in tables]
 
 
-def sample_kernel(slots, table, pushed, *, size):
+def sample_kernel(slots, table, pushed, filled, *, size):
     size_x, size_y, size_z = size
     planes = size_x * size_y
 
@@ -255,7 +259,7 @@
         tables = []
         for part in range(SAMPLE_GROUP):
             rows = slots[step * SAMPLE_GROUP + part]
-            shares, place_y, depth = marker_places(rows, size_x, size_y, size_z)
+            shares, place_y, depth = marker_places(*source_markers(rows), size_x, size_y, size_z)
             tables.append((rows, depth, marker_shares(shares, place_y, size_y)))
         depth = jnp.concatenate([entry[1] for entry in tables], axis=1)
         depth = jnp.concatenate([depth, depth], axis=0)
@@ -281,23 +285,72 @@
         return carry
 
     lax.fori_loop(0, slots.shape[0] // SAMPLE_GROUP, body, 0, unroll=SAMPLE_UNROLL)
+    most = [
+        jnp.max(slots[source, 8 * slot : 8 * slot + 8], axis=0, keepdims=True)
+        for source in range(slots.shape[0])
+        for slot in range(CAPB)
+    ]
+    most = jnp.max(jnp.concatenate(most, axis=0), axis=1, keepdims=True)
+    filled[...] = jnp.broadcast_to(jnp.where(most > 0.0, 1, 0), filled.shape)
 
 
 def spread_kernel(
-    place, slots, pushed, populations, collided, near_x, far_x, near_y, far_y, total
+    place,
+    slots,
+    pushed,
+    filled,
+    populations,
+    collided,
+    near_x,
+    far_x,
+    near_y,
+    far_y,
+    total,
+    held,
+    flags,
+    order,
+    sem,
 ):
     quantity, size_x, size_y, size_z = populations.shape
     planes = size_x * size_y
-    total[...] = jnp.zeros_like(total)
-
-    def body(step, carry):
+    copy = pltpu.make_async_copy(filled, flags, sem)
+    copy.start()
+    for x in range(size_x):
+        for y in range(0, size_y, CHUNK):
+            rows = slice(y, y + CHUNK)
+            current = [populations[q, x, rows] for q in range(quantity)]
+            density = sum_of(current)
+            held[0, x, rows] = density
+            held[1, x, rows] = 1.0 / density
+            for axis, value in enumerate(momentum_of(current)):
+                held[2 + axis, x, rows] = value
+
+    def whole_source(source):
+        both = pushed[source]
+        force = jnp.concatenate([both[0:4], both[4:8]], axis=1)
+        return (*source_markers(slots[source]), MARKER_AREA * force)
+
+    def one_slot(index, scale):
+        source = lax.shift_right_logical(index, 1)
+        slot = index & 1
+        weight = slots[source, pl.ds(pl.multiple_of(8 * slot, 8), 8), :]
+        tail = slots[source, 16:24, :]
+        both = pushed[source]
+        cell = jnp.where(slot == 0, tail[3:4], tail[7:8]).astype(jnp.int32)
+        return cell, weight, scale * jnp.where(slot == 0, both[0:4], both[4:8])
+
+    def listed_pair(number):
+        parts = []
+        for which in (number * 2, number * 2 + 1):
+            index = jnp.where(which < count, order[which], 0)
+            parts.append(one_slot(index, jnp.where(which < count, MARKER_AREA, 0.0)))
+        return tuple(jnp.concatenate(pair, axis=1) for pair in zip(*parts))
+
+    def spread(markers):
         wide, thin, strong, weak = [], [], [], []
-        for part in range(SPREAD_GROUP):
-            source = step * SPREAD_GROUP + part
-            shares, place_y, depth = marker_places(slots[source], size_x, size_y, size_z)
+        for cells, weight, force in markers:
+            shares, place_y, depth = marker_places(cells, weight, size_x, size_y, size_z)
             first, second = marker_halves(shares, place_y, size_y)
-            both = pushed[source]
-            force = MARKER_AREA * jnp.concatenate([both[0:4], both[4:8]], axis=1)
             high, low = halves(force)
             wide.append(first)
             thin.append(second)
@@ -311,10 +364,29 @@
         )
         rest = lax.dot_general(strong, thin, NT, preferred_element_type=F32)
         height = strong.shape[0]
-        total[...] += most[:height] + (most[height:] + rest)
-        return carry
-
-    lax.fori_loop(0, slots.shape[0] // SPREAD_GROUP, body, 0, unroll=SPREAD_UNROLL)
+        return most[:height] + (most[height:] + rest)
+
+    def repeat(group, steps, markers):
+        def body(step, carry):
+            total[...] += spread([markers(step * group + part) for part in range(group)])
+            return carry
+
+        lax.fori_loop(0, steps, body, 0, unroll=steps)
+
+    total[...] = jnp.zeros_like(total)
+    copy.wait()
+    count = jnp.int32(0)
+    for slot in range(flags.shape[0]):
+        order[count] = slot
+        count = count + flags[slot, 0]
+
+    @pl.when(count <= 2 * SPREAD_FEW)
+    def _():
+        repeat(SPREAD_FEW_GROUP, SPREAD_FEW // SPREAD_FEW_GROUP, listed_pair)
+
+    @pl.when(count > 2 * SPREAD_FEW)
+    def _():
+        repeat(SPREAD_GROUP, slots.shape[0] // SPREAD_GROUP, whole_source)
 
     for axis in range(3):
         span = slice(axis * size_z, (axis + 1) * size_z)
@@ -326,9 +398,9 @@
         for y in range(0, size_y, CHUNK):
             rows = slice(y, y + CHUNK)
             current = [populations[q, x, rows] for q in range(quantity)]
-            density = sum_of(current)
-            inverse = 1.0 / density
-            momentum = momentum_of(current)
+            density = held[0, x, rows]
+            inverse = held[1, x, rows]
+            momentum = [held[2 + axis, x, rows] for axis in range(3)]
             forcing = []
             for axis in range(3):
                 first = axis * size_z + x * size_y + y
@@ -583,11 +655,14 @@
         name="moments",
     )(populations, bond_pairs, bond_rest, grain_position, grain_motion)
 
-    pushed = pl.pallas_call(
+    pushed, filled = pl.pallas_call(
         lambda *refs: sample_kernel(*refs, size=(size_x, size_y, size_z)),
-        out_shape=shape((bricks, BACK_ROWS, MARKS), F32),
+        out_shape=[
+            shape((bricks, BACK_ROWS, MARKS), F32),
+            shape((bricks * CAPB, MARKS), jnp.int32),
+        ],
         in_specs=[VMEM] * 2,
-        out_specs=VMEM,
+        out_specs=[VMEM] * 2,
         compiler_params=params,
         name="sample",
     )(slots, table)
@@ -602,15 +677,21 @@
             shape((EDGE_ROWS, size_z), F32),
             shape((EDGE_ROWS, size_z), F32),
         ],
-        in_specs=[VMEM] * 4,
+        in_specs=[VMEM] * 5,
         out_specs=[VMEM] * 5,
-        scratch_shapes=[pltpu.VMEM((3 * size_z, 2 * planes), F32)],
+        scratch_shapes=[
+            pltpu.VMEM((3 * size_z, 2 * planes), F32),
+            pltpu.VMEM((5, size_x, size_y, size_z), F32),
+            pltpu.SMEM((bricks * CAPB, MARKS), jnp.int32),
+            pltpu.SMEM((bricks * CAPB + 1,), jnp.int32),
+            pltpu.SemaphoreType.DMA,
+        ],
         compiler_params=params,
         cost_estimate=pl.CostEstimate(
             flops=6000000000, bytes_accessed=8000000, transcendentals=0
         ),
         name="spread",
-    )(place, slots, pushed, populations)
+    )(place, slots, pushed, filled, populations)
 
     partial = pl.pallas_call(
         grain_kernel,

time: 69 us -> 67.2 us (0.974)
  Pallas kernels: 17.3 us -> 15.7 us
    pallas_call x1, Pallas kernels: 6.52 us -> 4.85 us  [shards(): pl.pallas_call(spread_kernel, out_shape=[shape(populations.shape, F32), s...]
  transfers between devices with their start and end apart: 8 -> 8, of which waited for: 4 -> 4; matrix products, arithmetic and copies ran while one was open for 0% -> 0% of each run, Pallas kernels for 14% -> 12%
where the time goes in v4:
time: 67.2 us; the launch traced here: 66.1 us
  starting transfers between devices  29.1 us (43%)
  waiting for transfers between devices  20.3 us (30%)
  Pallas kernels  15.7 us (23%)
  between operations  0.81 us (1%)
    all_to_all x1, waiting for transfers between devices, shards(): lax.all_to_all(outgoing, 'gx', split_axis=0, concat_axis=0, tiled=True)  13.3 us
    all_to_all x1, starting transfers between devices, shards(): lax.all_to_all(outgoing, 'gx', split_axis=0, concat_axis=0, tiled=True)  7.19 us
    ppermute x1, starting transfers between devices, shards(): far_y = lax.ppermute(far_y, 'gy', swap('gy', 1))  5.96 us
    ppermute x1, starting transfers between devices, shards(): far_x = lax.ppermute(faces[1], 'gx', swap('gx', 1))  5.69 us
    pallas_call x1, Pallas kernels, shards(): pl.pallas_call(lambda *refs: sample_kernel(*refs, size=(size_x, size_y, s...  5.36 us
    pallas_call x1, Pallas kernels, shards(): pl.pallas_call(spread_kernel, out_shape=[shape(populations.shape, F32), s...  4.85 us
    ppermute x1, starting transfers between devices, shards(): across = lax.ppermute(partial, 'gy', cross(4))  4.56 us
    all_to_all x1, starting transfers between devices, shards(): lax.all_to_all(pushed, 'gx', split_axis=0, concat_axis=0, tiled=True)  3.86 us
  transfers between devices with their start and end apart: 8, of which 4 were waited for; matrix products, arithmetic and copies ran while one was open for 0% of the time, Pallas kernels for 12%

profile of v4, /device:TPU:0, one launch (start us, length us, event | category | flops | bytes accessed | tf_op | source)
XLA Modules:
  0.0 66.1 jit_solution(11770786122638780548)
XLA Ops:
  0.6 0.0 copy-start.2
  0.6 0.0 copy-start
  0.7 0.0 copy-start.6
  0.7 2.1 %pack.1 = f32[32,24,128]{2,1,0:T(8,128)} custom-call(s32[16]{0:T(128)} %dest.1, s32[16,128]{1,0:T(8,128)} %bitcast.2, s32[16,128]{1,0:T(8,128)} %bitcast.4, f32[6,256]{1,0:T(8,128)} %motion.1, f32[3,2048]{1,0:T(4,128)} %offset.1, f32[8,2048]{1,0:T(8,128)} %refs_5_.1), custom_call_target="tpu_custom_call" | custom-call | tf_op jit(solution)/shard_map/pack/pallas_call | solution.py:616
  2.8 7.2 %all-to-all-start = ((f32[32,24,128]{2,1,0:T(8,128)}), f32[32,24,128]{2,1,0:T(8,128)S(1)}, u32[]{:S(2)}, u32[]{:S(2)}) async-start(f32[32,24,128]{2,1,0:T(8,128)} %pack.1), calls=%async_computation | async-start | bytes 786432 | tf_op jit(solution)/shard_map/all_to_all | solution.py:646
  10.0 0.0 copy-done.2
  10.0 0.0 copy-done
  10.0 0.0 copy-done.6
  10.0 0.0 copy-done.5
  10.1 0.0 copy-done.4
  10.1 0.6 moments.1
  10.6 13.3 %all-to-all-done.refs_0_.slots = f32[32,24,128]{2,1,0:T(8,128)S(1)} async-done(((f32[32,24,128]{2,1,0:T(8,128)}), f32[32,24,128]{2,1,0:T(8,128)S(1)}, u32[]{:S(2)}, u32[]{:S(2)}) %all-to-all-start) | async-done | bytes 393248 | tf_op jit(solution)/shard_map/all_to_all | solution.py:646
  23.9 5.4 %sample.1 = (f32[32,8,128]{2,1,0:T(8,128)}, s32[64,128]{1,0:T(8,128)S(1)}) custom-call(f32[32,24,128]{2,1,0:T(8,128)S(1)} %all-to-all-done.refs_0_.slots, bf16[768,256]{1,0:T(8,128)(2,1)S(1)} %get-tuple-element.14.refs_1_), custom_call_target="tpu_custom_call" | custom-call | tf_op jit(solution)/shard_map/sample/pallas_call | solution.py:658
  29.3 3.9 %all-to-all-start.1 = ((f32[32,8,128]{2,1,0:T(8,128)}), f32[32,8,128]{2,1,0:T(8,128)S(1)}, u32[]{:S(2)}, u32[]{:S(2)}) async-start(f32[32,8,128]{2,1,0:T(8,128)} %get-tuple-element.15.pushed), calls=%async_computation.1 | async-start | bytes 262144 | tf_op jit(solution)/shard_map/all_to_all | solution.py:669
  33.1 0.1 concatenate.6.place.refs_0_
  33.2 4.8 %spread.1 = (f32[19,4,32,128]{3,2,1,0:T(8,128)S(1)}, f32[5,32,128]{2,1,0:T(8,128)S(1)}, f32[5,32,128]{2,1,0:T(8,128)S(1)}, f32[24,128]{1,0:T(8,128)S(1)}, f32[24,128]{1,0:T(8,128)S(1)}) custom-call(s32[16,128]{1,0:T(8,128)S(1)} %concatenate.6.place.refs_0_, f32[32,24,128]{2,1,0:T(8,128)S(1)} %all-to-all-done.refs_0_.slots, ...), custom_call_target="tpu_custom_call" | custom-call | flops 6000000000 | bytes 8000000 | tf_op jit(solution)/shard_map/spread/pallas_call | solution.py:671
  38.1 0.3 collective-permute-start
  38.3 5.7 %collective-permute-start.1 = (f32[5,32,128]{2,1,0:T(8,128)S(1)}, f32[5,32,128]{2,1,0:T(8,128)S(1)}, u32[]{:S(2)}, u32[]{:S(2)}) collective-permute-start(f32[5,32,128]{2,1,0:T(8,128)S(1)} %get-tuple-element.19), channel_id=1, source_target_pairs={{0,248},{8,16},{16,8},{24,32},{32,24},{40,48},{48,40},{56,64},{64,... | collective-permute-start | bytes 245768 | tf_op jit(solution)/shard_map/ppermute | solution.py:706
  44.0 0.0 all-to-all-done.1.returned
  44.1 1.0 %grain.1.refs_5_ = f32[8,256]{1,0:T(8,128)S(1)} custom-call(s32[16]{0:T(128)S(1)} %copy-done.7, s32[16,128]{1,0:T(8,128)S(1)} %bitcast.3, f32[3,2048]{1,0:T(4,128)S(1)} %copy-done.1, f32[32,8,128]{2,1,0:T(8,128)S(1)} %all-to-all-done.1.returned, f32[24,128]{1,0:T(8,128)S(1)} %get-tuple-element.20.after.refs_3_), custom_call_target="tpu_custom_call" | custom-call | tf_op jit(solution)/shard_map/grain/pallas_call | solution.py:696
  45.1 4.6 %collective-permute-start.2 = (f32[8,256]{1,0:T(8,128)S(1)}, f32[8,256]{1,0:T(8,128)S(1)}, u32[]{:S(2)}, u32[]{:S(2)}) collective-permute-start(f32[8,256]{1,0:T(8,128)S(1)} %grain.1.refs_5_), channel_id=1, source_target_pairs={{0,4},{1,5},{2,6},{3,7},{4,0},{5,1},{6,2},{7,3},{8,12},{9,13},{10,... | collective-permute-start | bytes 24584 | tf_op jit(solution)/shard_map/ppermute | solution.py:707
  49.7 0.0 collective-permute-done.refs_1_.near_x
  49.7 0.0 collective-permute-done.1.refs_2_.far_x
  49.7 3.1 %collective-permute-done.2.refs_6_ = f32[8,256]{1,0:T(8,128)S(1)} collective-permute-done((f32[8,256]{1,0:T(8,128)S(1)}, f32[8,256]{1,0:T(8,128)S(1)}, u32[]{:S(2)}, u32[]{:S(2)}) %collective-permute-start.2) | collective-permute-done | bytes 8224 | tf_op jit(solution)/shard_map/ppermute | solution.py:707
  52.8 1.6 %collective-permute-start.3 = (f32[40,128]{1,0:T(8,128)S(1)}, f32[40,128]{1,0:T(8,128)S(1)}, u32[]{:S(2)}, u32[]{:S(2)}) collective-permute-start(f32[40,128]{1,0:T(8,128)S(1)} %get-tuple-element.22), channel_id=1, source_target_pairs={{0,1},{1,0},{2,3},{3,2},{4,5},{5,4},{6,7},{7,6},{8,9},{9,8},{10,11... | collective-permute-start | bytes 61448 | tf_op jit(solution)/shard_map/ppermute | solution.py:720
  54.4 6.0 %collective-permute-start.4 = (f32[24,128]{1,0:T(8,128)S(1)}, f32[24,128]{1,0:T(8,128)S(1)}, u32[]{:S(2)}, u32[]{:S(2)}) collective-permute-start(f32[24,128]{1,0:T(8,128)S(1)} %get-tuple-element.23), channel_id=1, source_target_pairs={{0,7},{1,2},{2,1},{3,4},{4,3},{5,6},{6,5},{7,0},{8,15},{9,10},{10,... | collective-permute-start | bytes 36872 | tf_op jit(solution)/shard_map/ppermute | solution.py:721
  60.3 0.0 collective-permute-done.3.near_y
  60.3 0.0 collective-permute-start.5
  60.4 3.8 %collective-permute-done.4.far_y = f32[24,128]{1,0:T(8,128)S(1)} collective-permute-done((f32[24,128]{1,0:T(8,128)S(1)}, f32[24,128]{1,0:T(8,128)S(1)}, u32[]{:S(2)}, u32[]{:S(2)}) %collective-permute-start.4) | collective-permute-done | bytes 12320 | tf_op jit(solution)/shard_map/ppermute | solution.py:721
  64.1 1.2 %stream.1 = f32[19,4,32,128]{3,2,1,0:T(8,128)} custom-call(s32[16,128]{1,0:T(8,128)S(1)} %concatenate.6.place.refs_0_, f32[19,4,32,128]{3,2,1,0:T(8,128)S(1)} %get-tuple-element.17.collided, f32[5,32,128]{2,1,0:T(8,128)S(1)} %collective-permute-done.refs_1_.near_x, f32[5,32,128]{2,1,0:T(8,128)S(1)} %collective-permute-done.1.refs_2_.far_x, ...), custom_call_target="tpu_custom_call" | custom-call | flops 20000000 | bytes 4000000 | tf_op jit(solution)/shard_map/stream/pallas_call | solution.py:731
  65.3 0.2 collective-permute-done.5.second
  65.5 0.6 load.1
  (12 shorter events, 0.0 us)
Async XLA Ops:
  0.6 9.4 %copy-start.2 = (f32[6,256]{1,0:T(8,128)S(1)}, f32[6,256]{1,0:T(8,128)}, u32[]{:S(2)}) copy-start(f32[6,256]{1,0:T(8,128)} %motion.1) | copy-start | bytes 18436
  0.6 9.4 %copy-start = (f32[19,4,32,128]{3,2,1,0:T(8,128)S(1)}, f32[19,4,32,128]{3,2,1,0:T(8,128)}, u32[]{:S(2)}) copy-start(f32[19,4,32,128]{3,2,1,0:T(8,128)} %populations.3) | copy-start | bytes 3735556
  0.7 9.4 %copy-start.6 = (f32[3,256]{1,0:T(4,128)S(1)}, f32[3,256]{1,0:T(4,128)}, u32[]{:S(2)}) copy-start(f32[3,256]{1,0:T(4,128)} %position.1) | copy-start | bytes 9220
  0.7 9.4 %copy-start.5 = (s32[2,512]{1,0:T(2,128)S(1)}, s32[2,512]{1,0:T(2,128)}, u32[]{:S(2)}) copy-start(s32[2,512]{1,0:T(2,128)} %pairs.1) | copy-start | bytes 12292
  0.7 9.4 %copy-start.4 = (f32[3,512]{1,0:T(4,128)S(1)}, f32[3,512]{1,0:T(4,128)}, u32[]{:S(2)}) copy-start(f32[3,512]{1,0:T(4,128)} %rest.1) | copy-start | bytes 18436
  2.8 21.1 %all-to-all-start = ((f32[32,24,128]{2,1,0:T(8,128)}), f32[32,24,128]{2,1,0:T(8,128)S(1)}, u32[]{:S(2)}, u32[]{:S(2)}) async-start(f32[32,24,128]{2,1,0:T(8,128)} %pack.1), calls=%async_computation | async-start | bytes 786432 | tf_op jit(solution)/shard_map/all_to_all | solution.py:646
  29.3 14.8 %all-to-all-start.1 = ((f32[32,8,128]{2,1,0:T(8,128)}), f32[32,8,128]{2,1,0:T(8,128)S(1)}, u32[]{:S(2)}, u32[]{:S(2)}) async-start(f32[32,8,128]{2,1,0:T(8,128)} %get-tuple-element.15.pushed), calls=%async_computation.1 | async-start | bytes 262144 | tf_op jit(solution)/shard_map/all_to_all | solution.py:669
  33.2 10.9 %copy-start.1 = (f32[3,2048]{1,0:T(4,128)S(1)}, f32[3,2048]{1,0:T(4,128)}, u32[]{:S(2)}) copy-start(f32[3,2048]{1,0:T(4,128)} %offset.1) | copy-start | bytes 73732
  33.2 10.9 %copy-start.3 = (s32[2048]{0:T(1024)S(1)}, s32[2048]{0:T(1024)}, u32[]{:S(2)}) copy-start(s32[2048]{0:T(1024)} %param.13) | copy-start | bytes 24580
  33.2 10.9 %copy-start.7 = (s32[16]{0:T(128)S(1)}, s32[16]{0:T(128)}, u32[]{:S(2)}) copy-start(s32[16]{0:T(128)} %dest.1) | copy-start | bytes 196
  38.1 11.6 %collective-permute-start = (f32[5,32,128]{2,1,0:T(8,128)S(1)}, f32[5,32,128]{2,1,0:T(8,128)S(1)}, u32[]{:S(2)}, u32[]{:S(2)}) collective-permute-start(f32[5,32,128]{2,1,0:T(8,128)S(1)} %get-tuple-element.18), channel_id=1, source_target_pairs={{0,8},{8,0},{16,24},{24,16},{32,40},{40,32},{48,56},{56,48},{64,72... | collective-permute-start | bytes 245768 | tf_op jit(solution)/shard_map/ppermute | solution.py:705
  38.3 11.3 %collective-permute-start.1 = (f32[5,32,128]{2,1,0:T(8,128)S(1)}, f32[5,32,128]{2,1,0:T(8,128)S(1)}, u32[]{:S(2)}, u32[]{:S(2)}) collective-permute-start(f32[5,32,128]{2,1,0:T(8,128)S(1)} %get-tuple-element.19), channel_id=1, source_target_pairs={{0,248},{8,16},{16,8},{24,32},{32,24},{40,48},{48,40},{56,64},{64,... | collective-permute-start | bytes 245768 | tf_op jit(solution)/shard_map/ppermute | solution.py:706
  45.1 7.7 %collective-permute-start.2 = (f32[8,256]{1,0:T(8,128)S(1)}, f32[8,256]{1,0:T(8,128)S(1)}, u32[]{:S(2)}, u32[]{:S(2)}) collective-permute-start(f32[8,256]{1,0:T(8,128)S(1)} %grain.1.refs_5_), channel_id=1, source_target_pairs={{0,4},{1,5},{2,6},{3,7},{4,0},{5,1},{6,2},{7,3},{8,12},{9,13},{10,... | collective-permute-start | bytes 24584 | tf_op jit(solution)/shard_map/ppermute | solution.py:707
  52.8 7.5 %collective-permute-start.3 = (f32[40,128]{1,0:T(8,128)S(1)}, f32[40,128]{1,0:T(8,128)S(1)}, u32[]{:S(2)}, u32[]{:S(2)}) collective-permute-start(f32[40,128]{1,0:T(8,128)S(1)} %get-tuple-element.22), channel_id=1, source_target_pairs={{0,1},{1,0},{2,3},{3,2},{4,5},{5,4},{6,7},{7,6},{8,9},{9,8},{10,11... | collective-permute-start | bytes 61448 | tf_op jit(solution)/shard_map/ppermute | solution.py:720
  54.4 9.8 %collective-permute-start.4 = (f32[24,128]{1,0:T(8,128)S(1)}, f32[24,128]{1,0:T(8,128)S(1)}, u32[]{:S(2)}, u32[]{:S(2)}) collective-permute-start(f32[24,128]{1,0:T(8,128)S(1)} %get-tuple-element.23), channel_id=1, source_target_pairs={{0,7},{1,2},{2,1},{3,4},{4,3},{5,6},{6,5},{7,0},{8,15},{9,10},{10,... | collective-permute-start | bytes 36872 | tf_op jit(solution)/shard_map/ppermute | solution.py:721
  60.3 5.2 %collective-permute-start.5 = (f32[8,256]{1,0:T(8,128)S(1)}, f32[8,256]{1,0:T(8,128)S(1)}, u32[]{:S(2)}, u32[]{:S(2)}) collective-permute-start(f32[8,256]{1,0:T(8,128)S(1)} %pair.1.first), channel_id=1, source_target_pairs={{0,2},{1,3},{2,0},{3,1},{4,6},{5,7},{6,4},{7,5},{8,10},{9,11},{10,... | collective-permute-start | bytes 24584 | tf_op jit(solution)/shard_map/ppermute | solution.py:752

commit v5 on v4

--- a/solution.py
+++ b/solution.py
@@ -13,8 +13,8 @@
 SAMPLE_GROUP = 2
 SAMPLE_UNROLL = 16
 SPREAD_GROUP = 8
-SPREAD_FEW = 12
-SPREAD_FEW_GROUP = 6
+SPREAD_FEW = 14
+SPREAD_FEW_GROUP = 7
 CHUNK = 8
 
 
@@ -558,7 +558,8 @@
     load[...] = total[: load.shape[0]]
 
 
-def grain_kernel(dest, grain, offset, returned, after, partial, used):
+def grain_kernel(dest, grain, offset, returned, face, partial, passed, used):
+    passed[...] = face[...]
     blocks = grain.shape[0]
     slab = partial.shape[1]
     for brick in range(returned.shape[0]):
@@ -693,16 +694,16 @@
         name="spread",
     )(place, slots, pushed, filled, populations)
 
-    partial = pl.pallas_call(
+    partial, near_face = pl.pallas_call(
         grain_kernel,
-        out_shape=shape((8, slab), F32),
-        in_specs=[SMEM] + [VMEM] * 3 + [HBM],
-        out_specs=VMEM,
+        out_shape=[shape((8, slab), F32), shape(faces[0].shape, F32)],
+        in_specs=[SMEM] + [VMEM] * 4,
+        out_specs=[VMEM] * 2,
         scratch_shapes=[pltpu.SMEM((bricks,), jnp.int32)],
         compiler_params=params,
         name="grain",
-    )(block_dest, grain_blocks, marker_offset, returned, faces[2])
-    near_x = lax.ppermute(faces[0], "gx", swap("gx", 0))
+    )(block_dest, grain_blocks, marker_offset, returned, faces[0])
+    near_x = lax.ppermute(near_face, "gx", swap("gx", 0))
     far_x = lax.ppermute(faces[1], "gx", swap("gx", 1))
     across = lax.ppermute(partial, "gy", cross(4))
     near_y, far_y, total = pl.pallas_call(

time: 67.2 us -> 67.3 us (level)
  no operation moved by 1% of the time
where the time goes in v5:
time: 67.3 us; the launch traced here: 66.2 us
  starting transfers between devices  28.9 us (43%)
  waiting for transfers between devices  20.3 us (30%)
  Pallas kernels  16 us (24%)
  between operations  0.82 us (1%)
    all_to_all x1, waiting for transfers between devices, shards(): lax.all_to_all(outgoing, 'gx', split_axis=0, concat_axis=0, tiled=True)  13.3 us
    all_to_all x1, starting transfers between devices, shards(): lax.all_to_all(outgoing, 'gx', split_axis=0, concat_axis=0, tiled=True)  7.19 us
    ppermute x1, starting transfers between devices, shards(): far_y = lax.ppermute(far_y, 'gy', swap('gy', 1))  6.02 us
    ppermute x1, starting transfers between devices, shards(): far_x = lax.ppermute(faces[1], 'gx', swap('gx', 1))  5.62 us
    pallas_call x1, Pallas kernels, shards(): pl.pallas_call(lambda *refs: sample_kernel(*refs, size=(size_x, size_y, s...  5.36 us
    pallas_call x1, Pallas kernels, shards(): pl.pallas_call(spread_kernel, out_shape=[shape(populations.shape, F32), s...  5.17 us
    ppermute x1, starting transfers between devices, shards(): across = lax.ppermute(partial, 'gy', cross(4))  4.59 us
    all_to_all x1, starting transfers between devices, shards(): lax.all_to_all(pushed, 'gx', split_axis=0, concat_axis=0, tiled=True)  3.86 us
  transfers between devices with their start and end apart: 8, of which 4 were waited for; matrix products, arithmetic and copies ran while one was open for 0% of the time, Pallas kernels for 12%

profile of v5, /device:TPU:0, one launch (start us, length us, event | category | flops | bytes accessed | tf_op | source)
XLA Modules:
  0.0 66.2 jit_solution(1269150241629937252)
XLA Ops:
  0.6 0.0 copy-start.2
  0.6 0.0 copy-start
  0.7 0.0 copy-start.6
  0.7 0.0 copy-start.5
  0.7 0.0 copy-start.4
  0.7 2.1 %pack.1 = f32[32,24,128]{2,1,0:T(8,128)} custom-call(s32[16]{0:T(128)} %dest.1, s32[16,128]{1,0:T(8,128)} %bitcast.2, s32[16,128]{1,0:T(8,128)} %bitcast.4, f32[6,256]{1,0:T(8,128)} %motion.1, f32[3,2048]{1,0:T(4,128)} %offset.1, f32[8,2048]{1,0:T(8,128)} %refs_5_.1), custom_call_target="tpu_custom_call" | custom-call | tf_op jit(solution)/shard_map/pack/pallas_call | solution.py:617
  2.8 7.2 %all-to-all-start = ((f32[32,24,128]{2,1,0:T(8,128)}), f32[32,24,128]{2,1,0:T(8,128)S(1)}, u32[]{:S(2)}, u32[]{:S(2)}) async-start(f32[32,24,128]{2,1,0:T(8,128)} %pack.1), calls=%async_computation | async-start | bytes 786432 | tf_op jit(solution)/shard_map/all_to_all | solution.py:647
  10.0 0.0 copy-done.2
  10.0 0.0 copy-done
  10.1 0.6 moments.1
  10.6 13.3 %all-to-all-done.refs_0_.slots = f32[32,24,128]{2,1,0:T(8,128)S(1)} async-done(((f32[32,24,128]{2,1,0:T(8,128)}), f32[32,24,128]{2,1,0:T(8,128)S(1)}, u32[]{:S(2)}, u32[]{:S(2)}) %all-to-all-start) | async-done | bytes 393248 | tf_op jit(solution)/shard_map/all_to_all | solution.py:647
  23.9 5.4 %sample.1 = (f32[32,8,128]{2,1,0:T(8,128)}, s32[64,128]{1,0:T(8,128)S(1)}) custom-call(f32[32,24,128]{2,1,0:T(8,128)S(1)} %all-to-all-done.refs_0_.slots, bf16[768,256]{1,0:T(8,128)(2,1)S(1)} %get-tuple-element.16.refs_1_), custom_call_target="tpu_custom_call" | custom-call | tf_op jit(solution)/shard_map/sample/pallas_call | solution.py:659
  29.3 3.9 %all-to-all-start.1 = ((f32[32,8,128]{2,1,0:T(8,128)}), f32[32,8,128]{2,1,0:T(8,128)S(1)}, u32[]{:S(2)}, u32[]{:S(2)}) async-start(f32[32,8,128]{2,1,0:T(8,128)} %get-tuple-element.17.pushed), calls=%async_computation.1 | async-start | bytes 262144 | tf_op jit(solution)/shard_map/all_to_all | solution.py:670
  33.1 0.1 concatenate.6.place.refs_0_
  33.2 5.2 %spread.1 = (f32[19,4,32,128]{3,2,1,0:T(8,128)S(1)}, f32[5,32,128]{2,1,0:T(8,128)S(1)}, f32[5,32,128]{2,1,0:T(8,128)S(1)}, f32[24,128]{1,0:T(8,128)S(1)}, f32[24,128]{1,0:T(8,128)S(1)}) custom-call(s32[16,128]{1,0:T(8,128)S(1)} %concatenate.6.place.refs_0_, f32[32,24,128]{2,1,0:T(8,128)S(1)} %all-to-all-done.refs_0_.slots, ...), custom_call_target="tpu_custom_call" | custom-call | flops 6000000000 | bytes 8000000 | tf_op jit(solution)/shard_map/spread/pallas_call | solution.py:672
  38.4 5.6 %collective-permute-start.1 = (f32[5,32,128]{2,1,0:T(8,128)S(1)}, f32[5,32,128]{2,1,0:T(8,128)S(1)}, u32[]{:S(2)}, u32[]{:S(2)}) collective-permute-start(f32[5,32,128]{2,1,0:T(8,128)S(1)} %get-tuple-element.22), channel_id=1, source_target_pairs={{0,248},{8,16},{16,8},{24,32},{32,24},{40,48},{48,40},{56,64},{64,... | collective-permute-start | bytes 245768 | tf_op jit(solution)/shard_map/ppermute | solution.py:707
  44.0 0.0 all-to-all-done.1.returned
  44.0 0.0 copy-done.1
  44.0 1.0 %grain.1 = (f32[8,256]{1,0:T(8,128)S(1)}, f32[5,32,128]{2,1,0:T(8,128)S(1)}) custom-call(s32[16]{0:T(128)S(1)} %copy-done.7, s32[16,128]{1,0:T(8,128)S(1)} %bitcast.3, f32[3,2048]{1,0:T(4,128)S(1)} %copy-done.1, f32[32,8,128]{2,1,0:T(8,128)S(1)} %all-to-all-done.1.returned, f32[5,32,128]{2,1,0:T(8,128)S(1)} %get-tuple-element.20.face), custom_call_target="tpu_custom_call" | custom-call | tf_op jit(solution)/shard_map/grain/pallas_call | solution.py:697
  45.1 0.1 collective-permute-start
  45.1 4.6 %collective-permute-start.2 = (f32[8,256]{1,0:T(8,128)S(1)}, f32[8,256]{1,0:T(8,128)S(1)}, u32[]{:S(2)}, u32[]{:S(2)}) collective-permute-start(f32[8,256]{1,0:T(8,128)S(1)} %get-tuple-element.25.refs_5_), channel_id=1, source_target_pairs={{0,4},{1,5},{2,6},{3,7},{4,0},{5,1},{6,2},{7,3},{8,12},{9,13},{10,... | collective-permute-start | bytes 24584 | tf_op jit(solution)/shard_map/ppermute | solution.py:708
  49.7 0.0 collective-permute-done.1.refs_2_.far_x
  49.7 3.1 %collective-permute-done.2.refs_6_ = f32[8,256]{1,0:T(8,128)S(1)} collective-permute-done((f32[8,256]{1,0:T(8,128)S(1)}, f32[8,256]{1,0:T(8,128)S(1)}, u32[]{:S(2)}, u32[]{:S(2)}) %collective-permute-start.2) | collective-permute-done | bytes 8224 | tf_op jit(solution)/shard_map/ppermute | solution.py:708
  52.8 0.0 collective-permute-done.refs_1_.near_x
  52.8 1.6 %collective-permute-start.3 = (f32[40,128]{1,0:T(8,128)S(1)}, f32[40,128]{1,0:T(8,128)S(1)}, u32[]{:S(2)}, u32[]{:S(2)}) collective-permute-start(f32[40,128]{1,0:T(8,128)S(1)} %get-tuple-element.26), channel_id=1, source_target_pairs={{0,1},{1,0},{2,3},{3,2},{4,5},{5,4},{6,7},{7,6},{8,9},{9,8},{10,11... | collective-permute-start | bytes 61448 | tf_op jit(solution)/shard_map/ppermute | solution.py:721
  54.4 6.0 %collective-permute-start.4 = (f32[24,128]{1,0:T(8,128)S(1)}, f32[24,128]{1,0:T(8,128)S(1)}, u32[]{:S(2)}, u32[]{:S(2)}) collective-permute-start(f32[24,128]{1,0:T(8,128)S(1)} %get-tuple-element.27), channel_id=1, source_target_pairs={{0,7},{1,2},{2,1},{3,4},{4,3},{5,6},{6,5},{7,0},{8,15},{9,10},{10,... | collective-permute-start | bytes 36872 | tf_op jit(solution)/shard_map/ppermute | solution.py:722
  60.4 0.0 collective-permute-done.3.near_y
  60.4 0.0 collective-permute-start.5
  60.4 3.7 %collective-permute-done.4.far_y = f32[24,128]{1,0:T(8,128)S(1)} collective-permute-done((f32[24,128]{1,0:T(8,128)S(1)}, f32[24,128]{1,0:T(8,128)S(1)}, u32[]{:S(2)}, u32[]{:S(2)}) %collective-permute-start.4) | collective-permute-done | bytes 12320 | tf_op jit(solution)/shard_map/ppermute | solution.py:722
  64.1 1.2 %stream.1 = f32[19,4,32,128]{3,2,1,0:T(8,128)} custom-call(s32[16,128]{1,0:T(8,128)S(1)} %concatenate.6.place.refs_0_, f32[19,4,32,128]{3,2,1,0:T(8,128)S(1)} %get-tuple-element.19.collided, f32[5,32,128]{2,1,0:T(8,128)S(1)} %collective-permute-done.refs_1_.near_x, f32[5,32,128]{2,1,0:T(8,128)S(1)} %collective-permute-done.1.refs_2_.far_x, ...), custom_call_target="tpu_custom_call" | custom-call | flops 20000000 | bytes 4000000 | tf_op jit(solution)/shard_map/stream/pallas_call | solution.py:732
  65.3 0.3 collective-permute-done.5.second
  65.6 0.6 load.1
  (12 shorter events, 0.0 us)
Async XLA Ops:
  0.6 9.4 %copy-start.2 = (f32[6,256]{1,0:T(8,128)S(1)}, f32[6,256]{1,0:T(8,128)}, u32[]{:S(2)}) copy-start(f32[6,256]{1,0:T(8,128)} %motion.1) | copy-start | bytes 18436
  0.6 9.4 %copy-start = (f32[19,4,32,128]{3,2,1,0:T(8,128)S(1)}, f32[19,4,32,128]{3,2,1,0:T(8,128)}, u32[]{:S(2)}) copy-start(f32[19,4,32,128]{3,2,1,0:T(8,128)} %populations.3) | copy-start | bytes 3735556
  0.7 9.4 %copy-start.6 = (f32[3,256]{1,0:T(4,128)S(1)}, f32[3,256]{1,0:T(4,128)}, u32[]{:S(2)}) copy-start(f32[3,256]{1,0:T(4,128)} %position.1) | copy-start | bytes 9220
  0.7 9.4 %copy-start.5 = (s32[2,512]{1,0:T(2,128)S(1)}, s32[2,512]{1,0:T(2,128)}, u32[]{:S(2)}) copy-start(s32[2,512]{1,0:T(2,128)} %pairs.1) | copy-start | bytes 12292
  0.7 9.4 %copy-start.4 = (f32[3,512]{1,0:T(4,128)S(1)}, f32[3,512]{1,0:T(4,128)}, u32[]{:S(2)}) copy-start(f32[3,512]{1,0:T(4,128)} %rest.1) | copy-start | bytes 18436
  2.8 21.1 %all-to-all-start = ((f32[32,24,128]{2,1,0:T(8,128)}), f32[32,24,128]{2,1,0:T(8,128)S(1)}, u32[]{:S(2)}, u32[]{:S(2)}) async-start(f32[32,24,128]{2,1,0:T(8,128)} %pack.1), calls=%async_computation | async-start | bytes 786432 | tf_op jit(solution)/shard_map/all_to_all | solution.py:647
  29.3 14.7 %all-to-all-start.1 = ((f32[32,8,128]{2,1,0:T(8,128)}), f32[32,8,128]{2,1,0:T(8,128)S(1)}, u32[]{:S(2)}, u32[]{:S(2)}) async-start(f32[32,8,128]{2,1,0:T(8,128)} %get-tuple-element.17.pushed), calls=%async_computation.1 | async-start | bytes 262144 | tf_op jit(solution)/shard_map/all_to_all | solution.py:670
  33.2 10.8 %copy-start.1 = (f32[3,2048]{1,0:T(4,128)S(1)}, f32[3,2048]{1,0:T(4,128)}, u32[]{:S(2)}) copy-start(f32[3,2048]{1,0:T(4,128)} %offset.1) | copy-start | bytes 73732
  33.2 10.8 %copy-start.3 = (s32[2048]{0:T(1024)S(1)}, s32[2048]{0:T(1024)}, u32[]{:S(2)}) copy-start(s32[2048]{0:T(1024)} %param.13) | copy-start | bytes 24580
  33.2 10.8 %copy-start.7 = (s32[16]{0:T(128)S(1)}, s32[16]{0:T(128)}, u32[]{:S(2)}) copy-start(s32[16]{0:T(128)} %dest.1) | copy-start | bytes 196
  38.4 11.4 %collective-permute-start.1 = (f32[5,32,128]{2,1,0:T(8,128)S(1)}, f32[5,32,128]{2,1,0:T(8,128)S(1)}, u32[]{:S(2)}, u32[]{:S(2)}) collective-permute-start(f32[5,32,128]{2,1,0:T(8,128)S(1)} %get-tuple-element.22), channel_id=1, source_target_pairs={{0,248},{8,16},{16,8},{24,32},{32,24},{40,48},{48,40},{56,64},{64,... | collective-permute-start | bytes 245768 | tf_op jit(solution)/shard_map/ppermute | solution.py:707
  45.1 7.7 %collective-permute-start = (f32[5,32,128]{2,1,0:T(8,128)S(1)}, f32[5,32,128]{2,1,0:T(8,128)S(1)}, u32[]{:S(2)}, u32[]{:S(2)}) collective-permute-start(f32[5,32,128]{2,1,0:T(8,128)S(1)} %get-tuple-element.21), channel_id=1, source_target_pairs={{0,8},{8,0},{16,24},{24,16},{32,40},{40,32},{48,56},{56,48},{64,72... | collective-permute-start | bytes 245768 | tf_op jit(solution)/shard_map/ppermute | solution.py:706
  45.1 7.6 %collective-permute-start.2 = (f32[8,256]{1,0:T(8,128)S(1)}, f32[8,256]{1,0:T(8,128)S(1)}, u32[]{:S(2)}, u32[]{:S(2)}) collective-permute-start(f32[8,256]{1,0:T(8,128)S(1)} %get-tuple-element.25.refs_5_), channel_id=1, source_target_pairs={{0,4},{1,5},{2,6},{3,7},{4,0},{5,1},{6,2},{7,3},{8,12},{9,13},{10,... | collective-permute-start | bytes 24584 | tf_op jit(solution)/shard_map/ppermute | solution.py:708
  52.8 7.6 %collective-permute-start.3 = (f32[40,128]{1,0:T(8,128)S(1)}, f32[40,128]{1,0:T(8,128)S(1)}, u32[]{:S(2)}, u32[]{:S(2)}) collective-permute-start(f32[40,128]{1,0:T(8,128)S(1)} %get-tuple-element.26), channel_id=1, source_target_pairs={{0,1},{1,0},{2,3},{3,2},{4,5},{5,4},{6,7},{7,6},{8,9},{9,8},{10,11... | collective-permute-start | bytes 61448 | tf_op jit(solution)/shard_map/ppermute | solution.py:721
  54.4 9.7 %collective-permute-start.4 = (f32[24,128]{1,0:T(8,128)S(1)}, f32[24,128]{1,0:T(8,128)S(1)}, u32[]{:S(2)}, u32[]{:S(2)}) collective-permute-start(f32[24,128]{1,0:T(8,128)S(1)} %get-tuple-element.27), channel_id=1, source_target_pairs={{0,7},{1,2},{2,1},{3,4},{4,3},{5,6},{6,5},{7,0},{8,15},{9,10},{10,... | collective-permute-start | bytes 36872 | tf_op jit(solution)/shard_map/ppermute | solution.py:722
  60.4 5.2 %collective-permute-start.5 = (f32[8,256]{1,0:T(8,128)S(1)}, f32[8,256]{1,0:T(8,128)S(1)}, u32[]{:S(2)}, u32[]{:S(2)}) collective-permute-start(f32[8,256]{1,0:T(8,128)S(1)} %pair.1.first), channel_id=1, source_target_pairs={{0,2},{1,3},{2,0},{3,1},{4,6},{5,7},{6,4},{7,5},{8,10},{9,11},{10,... | collective-permute-start | bytes 24584 | tf_op jit(solution)/shard_map/ppermute | solution.py:753
